TPU v7x, 32 devices: a whole 2x2x4 slice. The times are simulated.
32 devices in a mesh: dp: 8 (over z, core), mp: 4 (over y, x).
Axes of the slice: x: 2, y: 2, z: 4, core: 2. Of those that a mesh axis runs over, the one named last changes fastest.
Arguments:
- activations: bfloat16 [8, 1024, 4096], P('dp'), may hold values from -6 to 6
- out_grads: bfloat16 [8, 1024, 8192], P('dp', None, 'mp'), may hold values from -0.1875 to 0.1875
- error_fb: bfloat16 [8, 4096, 8192], P('dp', None, 'mp'), may hold values from -6 to 6
- q_prev: float32 [8192, 128], P('mp'), may hold values from -0.0625 to 0.0625
Outputs:
- new_error: bfloat16 [8, 4096, 8192], P('dp', None, 'mp')
- q_new: float32 [8192, 128], P('mp')
All inputs are finite; a program needn't handle non-finite values.
Results may differ from a plain program's by a relative error of at most 0.001.
Values sent between devices are 32-bit elements; how exact they have to be, the bound alone decides.
No kernel may reach another device: no remote copies, remote signals or barrier semaphores. Data moves between devices by JAX's collectives and lax.ppermute only.
A program may use at most 128 MiB of HBM per device.

v0:
```python
import jax
import jax.numpy as jnp
from jax import lax
from jax.sharding import PartitionSpec as P


def orthonormal(p_part, gram):
    chol = jnp.linalg.cholesky(gram)
    return lax.linalg.triangular_solve(chol, p_part, left_side=False, lower=True, transpose_a=True)


def self_gram(p_part):
    return jnp.dot(p_part.T, p_part, precision=lax.Precision.HIGHEST)


def per_device(activations, out_grads, error_fb, q_prev):
    grad_full = lax.dot_general(
        activations[0], out_grads[0], (((0,), (0,)), ((), ())), preferred_element_type=jnp.float32
    )
    merged = grad_full + error_fb[0].astype(jnp.float32)
    p_local = jnp.dot(merged, q_prev, precision=lax.Precision.HIGHEST)
    p_sum = lax.psum(p_local, ("dp", "mp"))
    p_hat = orthonormal(p_sum, self_gram(p_sum))
    q_local = lax.dot_general(
        merged, p_hat, (((0,), (0,)), ((), ())), precision=lax.Precision.HIGHEST
    )
    q_new = lax.psum(q_local, "dp") / lax.axis_size("dp")
    approx = jnp.dot(p_hat, q_new.T, precision=lax.Precision.HIGHEST)
    new_error = (merged - approx).astype(jnp.bfloat16)[None]
    return (new_error, q_new)


def solution(mesh):
    placed = (P("dp", None, None), P("dp", None, "mp"), P("dp", None, "mp"), P("mp", None))
    return jax.shard_map(
        per_device,
        mesh=mesh,
        in_specs=placed,
        out_specs=(P("dp", None, "mp"), P("mp", None)),
        check_vma=False,
    )
```

profile of v0, /device:TPU:0, one launch (start us, length us, event | category | flops | bytes accessed | tf_op | source)
XLA Modules:
  0.0 392.1 jit_solution(7035112465852525251)
XLA Ops:
  7.2 0.0 copy-start
  7.2 0.0 all-reduce.3.cloned.1.call-start
  7.2 29.1 %convert_add_fusion = f32[4096,2048]{1,0:T(8,128)} fusion(bf16[1,4096,2048]{2,1,0:T(8,128)(2,1)} %param.6, bf16[1,1024,4096]{2,1,0:T(8,128)(2,1)} %param.4, bf16[1,1024,2048]{2,1,0:T(8,128)(2,1)} %param.5), kind=kOutput, calls=%fused_computation | convolution fusion | flops 17196646400 | bytes 62914560 | tf_op jit(solution)/shard_map/dot_general | solution.py:17
  36.3 0.0 copy-done
  36.3 31.0 %fusion.7 = f32[4096,128]{1,0:T(8,128)} fusion(f32[4096,2048]{1,0:T(8,128)} %convert_add_fusion, f32[2048,128]{1,0:T(8,128)S(1)} %copy-done), kind=kOutput, calls=%fused_computation.16 | convolution fusion | flops 12884901888 | bytes 36700160 | tf_op jit(solution)/shard_map/dot_general | solution.py:21
  67.3 0.0 all-reduce.3.cloned.1.call-update
  67.3 0.4 all-reduce.5.cloned.1.call-start
  67.8 136.2 %all-reduce.3.cloned.1.call-done = f32[4096,128]{1,0:T(8,128)} async-done(((f32[4096,128]{1,0:T(8,128)}), f32[4096,128]{1,0:T(8,128)}) %all-reduce.3.cloned.1.call-update) | async-done | bytes 2097168 | tf_op jit(solution)/shard_map/psum | solution.py:22
  204.0 5.7 %fusion.8 = f32[128,128]{1,0:T(8,128)S(1)} fusion(f32[4096,128]{1,0:T(8,128)} %all-reduce.3.cloned.1.call-done), kind=kOutput, calls=%fused_computation.17 | convolution fusion | flops 805306368 | bytes 2162688 | tf_op jit(solution)/shard_map/dot_general | solution.py:13
  209.6 0.1 copy.6
  209.7 11.7 %cholesky.16 = f32[128,128]{1,0:T(8,128)S(1)} custom-call(f32[128,128]{1,0:T(8,128)S(1)} %fusion.6), custom_call_target="Cholesky" | custom-call | tf_op jit(solution)/shard_map/jit(cholesky)/cholesky | solution.py:8
  221.5 0.6 compare_reduce_fusion
  222.1 0.7 fusion.3
  222.8 9.8 %custom-call.6 = f32[1,128,128]{1,2,0:T(8,128)S(1)} custom-call(f32[1,128,128]{2,1,0:T(8,128)S(1)} %fusion.3), custom_call_target="InvertDiagBlocksLowerTriangular" | custom-call | tf_op jit(solution)/shard_map/triangular_solve | solution.py:9
  232.6 3.4 fusion.4
  236.0 57.0 %fusion.9 = f32[2048,128]{1,0:T(8,128)} fusion(f32[4096,2048]{1,0:T(8,128)} %convert_add_fusion, f32[4096,128]{1,0:T(8,128)S(1)} %fusion.4), kind=kOutput, calls=%fused_computation.18 | convolution fusion | flops 12884901888 | bytes 36700160 | tf_op jit(solution)/shard_map/dot_general | solution.py:24
  293.0 0.0 all-reduce.5.cloned.1.call-update
  293.0 57.9 %all-reduce.5.cloned.1.call-done = f32[2048,128]{1,0:T(8,128)} async-done(((f32[2048,128]{1,0:T(8,128)}), f32[2048,128]{1,0:T(8,128)}) %all-reduce.5.cloned.1.call-update) | async-done | bytes 1048592 | tf_op jit(solution)/shard_map/psum | solution.py:27
  350.9 1.3 broadcast_multiply_fusion
  352.2 0.0 copy-start.2
  352.2 0.0 copy-start.1
  352.2 32.9 %fusion = bf16[1,4096,2048]{2,1,0:T(8,128)(2,1)} fusion(f32[4096,2048]{1,0:T(8,128)} %convert_add_fusion, f32[4096,128]{1,0:T(8,128)S(1)} %fusion.4, f32[2048,128]{1,0:T(8,128)S(1)} %broadcast_multiply_fusion), kind=kOutput, calls=%fused_computation.2 | convolution fusion | flops 12901679104 | bytes 53477376 | tf_op jit(solution)/shard_map/dot_general | solution.py:28
  385.1 0.0 copy-done.2
  385.1 0.0 copy-done.1
  (2 shorter events, 0.0 us)
Async XLA Ops:
  7.2 29.1 %copy-start = (f32[2048,128]{1,0:T(8,128)S(1)}, f32[2048,128]{1,0:T(8,128)}, u32[]{:S(2)}) copy-start(f32[2048,128]{1,0:T(8,128)} %param.7) | copy-start | bytes 3145732
  7.2 196.8 %all-reduce.3.cloned.1.call-start = ((), (), s32[]{:S(2)}) async-start(), calls=%async_computation | async-start | bytes 4194304 | tf_op jit(solution)/shard_map/psum | solution.py:22
  67.3 283.6 %all-reduce.5.cloned.1.call-start = ((), (), s32[]{:S(2)}) async-start(), calls=%async_computation.1 | async-start | bytes 2097152 | tf_op jit(solution)/shard_map/psum | solution.py:27
  352.2 32.9 %copy-start.2 = (f32[2048,128]{1,0:T(8,128)}, f32[2048,128]{1,0:T(8,128)S(1)}, u32[]{:S(2)}) copy-start(f32[2048,128]{1,0:T(8,128)S(1)} %broadcast_multiply_fusion) | copy-start | bytes 3145732
  352.2 32.9 %copy-start.1 = (f32[2048,128]{1,0:T(8,128)S(1)}, f32[2048,128]{1,0:T(8,128)}, u32[]{:S(2)}) copy-start(f32[2048,128]{1,0:T(8,128)} %param.7) | copy-start | bytes 3145732
Sparse Core Ops, SparseCore 0:
  67.5 136.4 all-reduce.2
  293.1 57.6 all-reduce.4
where the time goes:
time: 397 us; the launch traced here: 392 us
  waiting for transfers between devices  194 us (49%)
  matrix products  159 us (40%)
  other arithmetic  24.2 us (6%)
  between operations  14.3 us (4%)
    psum x1, waiting for transfers between devices, per_device(): p_sum = lax.psum(p_local, ('dp', 'mp'))  136 us
    psum x1, waiting for transfers between devices, per_device(): q_new = lax.psum(q_local, 'dp') / lax.axis_size('dp')  57.9 us
    dot_general x1, matrix products, per_device(): lax.dot_general(merged, p_hat, (((0,), (0,)), ((), ())), precision=lax.Pr...  57 us
    dot_general x1, matrix products, per_device(): approx = jnp.dot(p_hat, q_new.T, precision=lax.Precision.HIGHEST)  32.9 us
    dot_general x1, matrix products, per_device(): p_local = jnp.dot(merged, q_prev, precision=lax.Precision.HIGHEST)  31 us
    dot_general x1, matrix products, per_device(): lax.dot_general(activations[0], out_grads[0], (((0,), (0,)), ((), ())), p...  29.1 us
    another operation x3, other arithmetic, orthonormal(): chol = jnp.linalg.cholesky(gram)  12.4 us
    another operation x2, other arithmetic, orthonormal(): lax.linalg.triangular_solve(chol, p_part, left_side=False, lower=True, tr...  10.5 us
  transfers between devices with their start and end apart: 2, of which 2 were waited for; matrix products, arithmetic and copies ran while one was open for 0% of the time, Pallas kernels for 0%

commit v1 on v0

v1 whole, which is shorter than its diff:
```python
import functools

import jax
import jax.numpy as jnp
from jax import lax
from jax.experimental import pallas as pl
from jax.experimental.pallas import tpu as pltpu
from jax.sharding import PartitionSpec as P

F32 = jnp.float32
BF16 = jnp.bfloat16
HIGHEST = lax.Precision.HIGHEST
RANK = 128
VMEM_LIMIT = 50 * 1024 * 1024


def params(limit=VMEM_LIMIT):
    return pltpu.CompilerParams(vmem_limit_bytes=limit)


def cost(flops, nbytes):
    return pl.CostEstimate(flops=flops, bytes_accessed=nbytes, transcendentals=0)


def split(x):
    hi = x.astype(BF16)
    lo = (x - hi.astype(F32)).astype(BF16)
    return jnp.concatenate([hi, lo], axis=1)


def split_rows(x):
    hi = x.astype(BF16)
    lo = (x - hi.astype(F32)).astype(BF16)
    return jnp.concatenate([hi, lo], axis=0)


def halves(y):
    return y[:, :RANK] + y[:, RANK:]


def dot(a, b, contract=((1,), (0,))):
    return lax.dot_general(a, b, (contract, ((), ())), preferred_element_type=F32)


def u_kernel(g_ref, q_ref, ucat_ref, qcat_ref):
    @pl.when(pl.program_id(0) == 0)
    def _():
        qcat_ref[...] = split(q_ref[...])

    ucat_ref[...] = split(halves(dot(g_ref[...], qcat_ref[...])))


def grads_by_q(g, q):
    tok, cols = g.shape
    tile = tok // 4
    return pl.pallas_call(
        u_kernel,
        grid=(tok // tile,),
        in_specs=[
            pl.BlockSpec((tile, cols), lambda i: (i, 0)),
            pl.BlockSpec((cols, RANK), lambda i: (0, 0)),
        ],
        out_specs=[
            pl.BlockSpec((tile, 2 * RANK), lambda i: (i, 0)),
            pl.BlockSpec((cols, 2 * RANK), lambda i: (0, 0)),
        ],
        out_shape=[
            jax.ShapeDtypeStruct((tok, 2 * RANK), BF16),
            jax.ShapeDtypeStruct((cols, 2 * RANK), BF16),
        ],
        compiler_params=params(),
        cost_estimate=cost(4 * tok * cols * RANK, tok * cols * 2 + cols * RANK * 8),
        name="grads_by_q",
    )(g, q)


def p_kernel(nz, ids_ref, a_ref, e_ref, ucat_ref, qcat_ref, p_ref, acc_ref):
    acc = dot(e_ref[...], qcat_ref[...])
    acc += dot(a_ref[...], ucat_ref[...], ((0,), (0,)))
    acc_ref[...] = halves(acc)
    rows = p_ref.shape[2]
    for k in range(nz):
        start = pl.multiple_of((ids_ref[2] ^ k) * rows, rows)
        p_ref[0, k] = acc_ref[pl.ds(start, rows), :]


def left_terms(ids, a, e, ucat, qcat, kc, nm, nz):
    tok, rows = a.shape
    cols = e.shape[1]
    tile = rows // (2 * nm)

    def block(j, ids_ref):
        return (ids_ref[0] ^ kc) * nm + (ids_ref[1] ^ j)

    return pl.pallas_call(
        functools.partial(p_kernel, nz),
        grid_spec=pltpu.PrefetchScalarGridSpec(
            num_scalar_prefetch=1,
            grid=(nm,),
            in_specs=[
                pl.BlockSpec((tok, tile), lambda j, ids_ref: (0, block(j, ids_ref))),
                pl.BlockSpec((tile, cols), lambda j, ids_ref: (block(j, ids_ref), 0)),
                pl.BlockSpec((tok, 2 * RANK), lambda j, ids_ref: (0, 0)),
                pl.BlockSpec((cols, 2 * RANK), lambda j, ids_ref: (0, 0)),
            ],
            out_specs=pl.BlockSpec((1, nz, tile // nz, RANK), lambda j, ids_ref: (j, 0, 0, 0)),
            scratch_shapes=[pltpu.VMEM((tile, RANK), F32)],
        ),
        out_shape=jax.ShapeDtypeStruct((nm, nz, tile // nz, RANK), F32),
        compiler_params=params(),
        cost_estimate=cost(2 * rows * RANK * (tok + cols), rows * (tok + cols)),
        name="left_terms",
    )(ids, a, e, ucat, qcat)


def merged_kernel(first, *refs):
    a_ref, e_ref, g_ref, out_ref = refs if first else refs[1:]
    out_ref[...] = dot(a_ref[...], g_ref[...], ((0,), (0,))) + e_ref[...].astype(F32)


def merged_part(buf, a, e, g, part, parts):
    tok, rows = a.shape
    cols = e.shape[1]
    tile = rows // 8
    steps = rows // tile // parts
    first = buf is None
    specs = [
        pl.BlockSpec((tok, tile), lambda i: (0, part * steps + i)),
        pl.BlockSpec((tile, cols), lambda i: (part * steps + i, 0)),
        pl.BlockSpec((tok, cols), lambda i: (0, 0)),
    ]
    args = [a, e, g]
    if not first:
        specs = [pl.BlockSpec(memory_space=pl.ANY)] + specs
        args = [buf] + args
    return pl.pallas_call(
        functools.partial(merged_kernel, first),
        grid=(steps,),
        in_specs=specs,
        out_specs=pl.BlockSpec((tile, cols), lambda i: (part * steps + i, 0)),
        out_shape=jax.ShapeDtypeStruct((rows, cols), F32),
        input_output_aliases={} if first else {0: 0},
        compiler_params=params(),
        cost_estimate=cost(
            2 * tok * cols * rows // parts, (rows * cols * 6 + rows * tok * 2) // parts + tok * cols * 2
        ),
        name="merged",
    )(*args)


def q_kernel(nm, nz, last, ids_ref, *refs):
    pieces, refs = refs[:nm], refs[nm:]
    if last:
        v_in, q_in, a_ref, e_ref, g_ref, q_ref, pcat, pt, v_acc, q_acc = refs
    else:
        a_ref, e_ref, v_ref, q_ref, pcat, pt, v_acc, q_acc = refs
    j = pl.program_id(0)
    rows = pieces[0].shape[1]

    @pl.when(j == 0)
    def _():
        if last:
            v_acc[...] = v_in[...]
            q_acc[...] = q_in[...]
        else:
            v_acc[...] = jnp.zeros_like(v_acc)
            q_acc[...] = jnp.zeros_like(q_acc)

    for m in range(nm):

        @pl.when(j == m)
        def _():
            for k in range(nz):
                start = pl.multiple_of((ids_ref[2] ^ k) * rows, rows)
                pcat[pl.ds(start, rows), :] = split(pieces[m][k])

    v_acc[...] += halves(dot(a_ref[...], pcat[...]))
    both = dot(pcat[...], e_ref[...], ((0,), (0,)))
    q_acc[...] += both[:RANK] + both[RANK:]

    @pl.when(j == nm - 1)
    def _():
        if last:
            more = dot(split(v_acc[...]), g_ref[...], ((0,), (0,)))
            q_ref[...] = q_acc[...] + (more[:RANK] + more[RANK:])
        else:
            v_ref[...] = v_acc[...]
            q_ref[...] = q_acc[...]


def right_terms(ids, pieces, a, e, g, kc, before=None):
    tok, rows = a.shape
    cols = e.shape[1]
    nm = len(pieces)
    nz, small = pieces[0].shape[:2]
    tile = rows // (2 * nm)
    last = before is not None

    def block(j, ids_ref):
        return (ids_ref[0] ^ kc) * nm + (ids_ref[1] ^ j)

    whole = lambda *shape: pl.BlockSpec(shape, lambda j, ids_ref: (0,) * len(shape))
    specs = [whole(nz, small, RANK)] * nm
    args = list(pieces)
    if last:
        specs += [whole(tok, RANK), whole(RANK, cols)]
        args += list(before)
    specs += [
        pl.BlockSpec((tok, tile), lambda j, ids_ref: (0, block(j, ids_ref))),
        pl.BlockSpec((tile, cols), lambda j, ids_ref: (block(j, ids_ref), 0)),
    ]
    args += [a, e]
    if last:
        specs += [whole(tok, cols)]
        args += [g]
        out_specs = whole(RANK, cols)
        out_shape = jax.ShapeDtypeStruct((RANK, cols), F32)
    else:
        out_specs = [whole(tok, RANK), whole(RANK, cols)]
        out_shape = [jax.ShapeDtypeStruct((tok, RANK), F32), jax.ShapeDtypeStruct((RANK, cols), F32)]
    return pl.pallas_call(
        functools.partial(q_kernel, nm, nz, last),
        grid_spec=pltpu.PrefetchScalarGridSpec(
            num_scalar_prefetch=1,
            grid=(nm,),
            in_specs=specs,
            out_specs=out_specs,
            scratch_shapes=[
                pltpu.VMEM((tile, 2 * RANK), BF16),
                pltpu.VMEM((8, RANK), F32),
                pltpu.VMEM((tok, RANK), F32),
                pltpu.VMEM((RANK, cols), F32),
            ],
        ),
        out_shape=out_shape,
        compiler_params=params(),
        cost_estimate=cost(2 * rows * RANK * (tok + cols), rows * (tok + cols)),
        name="right_terms",
    )(ids, *args)


def p_hat_kernel(nm, nz, ids_ref, *refs):
    pieces, (linv_ref, out_ref) = refs[: 2 * nm], refs[2 * nm :]
    small = pieces[0].shape[1]
    for h in range(2):
        for m in range(nm):
            for k in range(nz):
                block = ((ids_ref[0] ^ h) * nm + (ids_ref[1] ^ m)) * nz + (ids_ref[2] ^ k)
                tile = lax.dot_general(
                    pieces[h * nm + m][k], linv_ref[...], (((1,), (1,)), ((), ())), precision=HIGHEST,
                    preferred_element_type=F32,
                )
                out_ref[pl.ds(pl.multiple_of(block * small, small), small), :] = split(tile)


def left_factor(ids, pieces, linv):
    nm = len(pieces) // 2
    nz, small = pieces[0].shape[:2]
    rows = 2 * nm * nz * small
    return pl.pallas_call(
        functools.partial(p_hat_kernel, nm, nz),
        grid_spec=pltpu.PrefetchScalarGridSpec(
            num_scalar_prefetch=1,
            grid=(),
            in_specs=[pl.BlockSpec(memory_space=pltpu.VMEM)] * (2 * nm + 1),
            out_specs=pl.BlockSpec(memory_space=pltpu.VMEM),
        ),
        out_shape=jax.ShapeDtypeStruct((rows, 2 * RANK), BF16),
        compiler_params=params(),
        cost_estimate=cost(12 * rows * RANK * RANK, rows * RANK * 8),
        name="left_factor",
    )(ids, *pieces, linv)


def final_kernel(nz, scale, ids_ref, *refs):
    pieces, (linv_ref, phat_ref, merged_ref, err_ref, qnew_ref, q_sum, q_hi, q_lo) = (
        refs[: 2 * nz],
        refs[2 * nz :],
    )
    small = pieces[0].shape[0]

    @pl.when(pl.program_id(0) == 0)
    def _():
        for h in range(2):
            for k in range(nz):
                block = (ids_ref[0] ^ h) * nz + (ids_ref[2] ^ k)
                q_sum[pl.ds(pl.multiple_of(block * small, small), small), :] = pieces[h * nz + k][...]
        q_t = lax.dot_general(
            linv_ref[...], q_sum[...], (((1,), (0,)), ((), ())), precision=HIGHEST, preferred_element_type=F32
        ) * scale
        qnew_ref[...] = q_t.T
        hi = q_t.astype(BF16)
        lo = (q_t - hi.astype(F32)).astype(BF16)
        q_hi[...] = jnp.concatenate([hi, hi], axis=0)
        q_lo[...] = jnp.concatenate([lo, lo], axis=0)

    approx = dot(phat_ref[...], q_hi[...]) + dot(phat_ref[...], q_lo[...])
    err_ref[0] = (merged_ref[...] - approx).astype(BF16)


def finish(ids, pieces, linv, phat, merged, replicas):
    nz = len(pieces) // 2
    rows, cols = merged.shape
    tile = rows // 8
    whole = lambda *shape: pl.BlockSpec(shape, lambda j, ids_ref: (0,) * len(shape))
    return pl.pallas_call(
        functools.partial(final_kernel, nz, 1.0 / replicas),
        grid_spec=pltpu.PrefetchScalarGridSpec(
            num_scalar_prefetch=1,
            grid=(rows // tile,),
            in_specs=[whole(*pieces[0].shape)] * (2 * nz)
            + [
                whole(RANK, RANK),
                pl.BlockSpec((tile, 2 * RANK), lambda j, ids_ref: (j, 0)),
                pl.BlockSpec((tile, cols), lambda j, ids_ref: (j, 0)),
            ],
            out_specs=[
                pl.BlockSpec((1, tile, cols), lambda j, ids_ref: (0, j, 0)),
                whole(cols, RANK),
            ],
            scratch_shapes=[
                pltpu.VMEM((RANK, cols), F32),
                pltpu.VMEM((2 * RANK, cols), BF16),
                pltpu.VMEM((2 * RANK, cols), BF16),
            ],
        ),
        out_shape=[jax.ShapeDtypeStruct((1, rows, cols), BF16), jax.ShapeDtypeStruct((cols, RANK), F32)],
        compiler_params=params(),
        cost_estimate=cost(8 * rows * cols * RANK, rows * cols * 6),
        name="new_error",
    )(ids, *pieces, linv, phat, merged)


def per_device(n_dp, n_mp, activations, out_grads, error_fb, q_prev):
    a, g, e = activations[0], out_grads[0], error_fb[0]
    nz = n_dp // 2
    dp, mp = lax.axis_index("dp"), lax.axis_index("mp")
    ids = jnp.stack([dp % 2, mp, dp // 2]).astype(jnp.int32)

    def to_core(x):
        return lax.ppermute(x, "dp", [(i, i ^ 1) for i in range(n_dp)])

    def to_z(x, k):
        return lax.ppermute(x, "dp", [(i, i ^ (2 * k)) for i in range(n_dp)])

    def to_mp(x, k):
        return lax.ppermute(x, "mp", [(i, i ^ k) for i in range(n_mp)])

    ucat, qcat = grads_by_q(g, q_prev)
    p_far = left_terms(ids, a, e, ucat, qcat, 1, n_mp, nz)
    p_arrived = to_core(p_far)
    p_near = left_terms(ids, a, e, ucat, qcat, 0, n_mp, nz)
    p1 = p_near + p_arrived
    p2 = p1[0] + sum(to_mp(p1[k], k) for k in range(1, n_mp))
    p3 = p2[0] + sum(to_z(p2[k], k) for k in range(1, nz))
    p4 = jnp.stack([p3] + [to_z(p3, k) for k in range(1, nz)])
    near = [p4] + [to_mp(p4, k) for k in range(1, n_mp)]
    far = [to_core(x) for x in near]

    merged = None
    for part in range(4):
        merged = merged_part(merged, a, e, g, part, 4)

    half = right_terms(ids, near, a, e, g, 0)
    q_local = right_terms(ids, far, a, e, g, 1, half)

    small = RANK // (2 * nz)
    c = dp % 2
    z = dp // 2
    q_blocks = q_local.reshape(2, nz, small, q_local.shape[1])
    q_mine = lax.dynamic_index_in_dim(q_blocks, c, 0, keepdims=False)
    q_far = lax.dynamic_index_in_dim(q_blocks, c ^ 1, 0, keepdims=False)
    q1 = q_mine + to_core(q_far)
    take = lambda k: lax.dynamic_index_in_dim(q1, z ^ k, 0, keepdims=False)
    q3 = take(0) + sum(to_z(take(k), k) for k in range(1, nz))
    q_near = [q3] + [to_z(q3, k) for k in range(1, nz)]
    q_pieces = q_near + [to_core(x) for x in q_near]

    p_all = jnp.concatenate([x.reshape(-1, RANK) for x in near + far])
    gram = lax.dot_general(p_all, p_all, (((0,), (0,)), ((), ())), precision=HIGHEST)
    chol = jnp.linalg.cholesky(gram)
    linv = lax.linalg.triangular_solve(chol, jnp.eye(RANK, dtype=F32), left_side=True, lower=True)
    phat = left_factor(ids, near + far, linv)
    new_error, q_new = finish(ids, q_pieces, linv, phat, merged, n_dp)
    return new_error, q_new


def solution(mesh):
    placed = (P("dp", None, None), P("dp", None, "mp"), P("dp", None, "mp"), P("mp", None))
    return jax.shard_map(
        functools.partial(per_device, mesh.shape["dp"], mesh.shape["mp"]),
        mesh=mesh,
        in_specs=placed,
        out_specs=(P("dp", None, "mp"), P("mp", None)),
        check_vma=False,
    )
```

time: 397 us -> 186 us (0.47); the launches traced: 392 us -> 186 us
  waiting for transfers between devices: 194 us -> 18.4 us
  matrix products: 159 us -> 3.83 us
  Pallas kernels: 0 us -> 107 us
  starting transfers between devices: 0.48 us -> 27.2 us
  between operations: 14.3 us -> 0.99 us
    psum x2 -> x0, waiting for transfers between devices: 194 us -> none  [the longest x1 136 us: per_device(): p_sum = lax.psum(p_local, ('dp', 'mp'))]
    dot_general x5 -> x1, matrix products: 156 us -> 3.58 us  [per_device(): lax.dot_general(p_all, p_all, (((0,), (0,)), ((), ())), precision=HIGHEST)]
    pallas_call x0 -> x11, Pallas kernels: none -> 107 us  [the longest x4 39.6 us: merged_part(): pl.pallas_call(functools.partial(merged_kernel, first), grid=(steps,), in...]
    ppermute x0 -> x28, starting transfers between devices: none -> 27.2 us  [the longest x12 16.9 us: to_z(): return lax.ppermute(x, 'dp', [(i, i ^ 2 * k) for i in range(n_dp)])]
    ppermute x0 -> x28, waiting for transfers between devices: none -> 18.4 us  [the longest x12 9.25 us: to_z(): return lax.ppermute(x, 'dp', [(i, i ^ 2 * k) for i in range(n_dp)])]
    another operation x5 -> x7, other arithmetic: 22.9 us -> 22.9 us  [the longest x3 12.4 us: per_device(): chol = jnp.linalg.cholesky(gram)]
  transfers between devices with their start and end apart: 2 -> 28, of which waited for: 2 -> 5; matrix products, arithmetic and copies ran while one was open for 0% -> 14% of each run, Pallas kernels for 0% -> 33%
where the time goes in v1:
time: 186 us
  Pallas kernels  107 us (58%)
  starting transfers between devices  27.2 us (15%)
  other arithmetic  24.3 us (13%)
  waiting for transfers between devices  18.4 us (10%)
  local copies, waits for them, and re-layouts  3.99 us (2%)
  matrix products  3.83 us (2%)
    pallas_call x4, Pallas kernels, merged_part(): pl.pallas_call(functools.partial(merged_kernel, first), grid=(steps,), in...  39.6 us
    pallas_call x1, Pallas kernels, finish(): pl.pallas_call(functools.partial(final_kernel, nz, 1.0 / replicas), grid_...  23.1 us
    pallas_call x2, Pallas kernels, right_terms(): pl.pallas_call(functools.partial(q_kernel, nm, nz, last), grid_spec=pltpu...  18.6 us
    ppermute x12, starting transfers between devices, to_z(): return lax.ppermute(x, 'dp', [(i, i ^ 2 * k) for i in range(n_dp)])  16.9 us
    pallas_call x2, Pallas kernels, left_terms(): pl.pallas_call(functools.partial(p_kernel, nz), grid_spec=pltpu.PrefetchS...  15.4 us
    another operation x3, other arithmetic, per_device(): chol = jnp.linalg.cholesky(gram)  12.4 us
    another operation x2, other arithmetic, per_device(): lax.linalg.triangular_solve(chol, jnp.eye(RANK, dtype=F32), left_side=Tru...  10.5 us
    ppermute x12, waiting for transfers between devices, to_z(): return lax.ppermute(x, 'dp', [(i, i ^ 2 * k) for i in range(n_dp)])  9.25 us
  transfers between devices with their start and end apart: 28, of which 5 were waited for; matrix products, arithmetic and copies ran while one was open for 14% of the time, Pallas kernels for 33%

profile of v1, /device:TPU:0, one launch (start us, length us, event | category | flops | bytes accessed | tf_op | source)
XLA Modules:
  0.0 186.0 jit_solution(4600766832682359852)
XLA Ops:
  0.7 1.2 copy-done.1
  1.9 4.1 %grads_by_q.1 = (bf16[1024,256]{1,0:T(8,128)(2,1)S(1)}, bf16[2048,256]{1,0:T(8,128)(2,1)S(1)}) custom-call(bf16[1024,2048]{1,0:T(8,128)(2,1)} %bitcast.88, f32[2048,128]{1,0:T(8,128)S(1)} %copy-done.1), custom_call_target="tpu_custom_call" | custom-call | flops 1073741824 | bytes 6291456 | tf_op jit(solution)/shard_map/grads_by_q/pallas_call | solution.py:56
  6.0 7.7 %left_terms.3 = f32[4,4,128,128]{3,2,1,0:T(8,128)S(1)} custom-call(s32[3]{0:T(128)S(1)} %pad_add_fusion.ids_ref, bf16[1024,4096]{1,0:T(8,128)(2,1)} %bitcast.80, bf16[4096,2048]{1,0:T(8,128)(2,1)} %bitcast.72, bf16[1024,256]{1,0:T(8,128)(2,1)S(1)} %get-tuple-element.6.ucat_ref, bf16[2048,256]{1,0:T(8,128)(2,1)S(1)} %get-tuple-element.7.qcat_ref), custom_call_target="tpu_custom_call" | custom-call | flops 3221225472 | bytes 12582912 | tf_op jit(solution)/shard_map/left_terms/pallas_call | solution.py:95
  13.7 0.5 collective-permute-start
  14.3 7.7 %left_terms.2 = f32[4,4,128,128]{3,2,1,0:T(8,128)S(1)} custom-call(s32[3]{0:T(128)S(1)} %pad_add_fusion.ids_ref, bf16[1024,4096]{1,0:T(8,128)(2,1)} %bitcast.81, bf16[4096,2048]{1,0:T(8,128)(2,1)} %bitcast.73, bf16[1024,256]{1,0:T(8,128)(2,1)S(1)} %get-tuple-element.6.ucat_ref, bf16[2048,256]{1,0:T(8,128)(2,1)S(1)} %get-tuple-element.7.qcat_ref), custom_call_target="tpu_custom_call" | custom-call | flops 3221225472 | bytes 12582912 | tf_op jit(solution)/shard_map/left_terms/pallas_call | solution.py:95
  22.2 2.6 %collective-permute-start.2 = (f32[4,128,128]{2,1,0:T(8,128)S(1)}, f32[4,128,128]{2,1,0:T(8,128)S(1)}, u32[]{:S(2)}, u32[]{:S(2)}) collective-permute-start(f32[4,128,128]{2,1,0:T(8,128)S(1)} %get-tuple-element.10), channel_id=1, source_target_pairs={{0,2},{1,3},{2,0},{3,1},{4,6},{5,7},{6,4},{7,5},{8,10},{9,11},{10,... | collective-permute-start | bytes 786440 | tf_op jit(solution)/shard_map/ppermute | solution.py:347
  24.8 1.4 collective-permute-start.3
  26.4 9.9 %merged.4.refs_0_ = f32[4096,2048]{1,0:T(8,128)} custom-call(bf16[1024,4096]{1,0:T(8,128)(2,1)} %bitcast.82, bf16[4096,2048]{1,0:T(8,128)(2,1)} %bitcast.74, bf16[1024,2048]{1,0:T(8,128)(2,1)} %bitcast.89), custom_call_target="tpu_custom_call" | custom-call | flops 4294967296 | bytes 18874368 | tf_op jit(solution)/shard_map/merged/pallas_call | solution.py:136
  36.3 1.1 collective-permute-done.2
  37.4 1.3 collective-permute-done.1
  38.8 2.8 %collective-permute-start.5 = (f32[128,128]{1,0:T(8,128)S(1)}, f32[128,128]{1,0:T(8,128)S(1)}, u32[]{:S(2)}, u32[]{:S(2)}) collective-permute-start(f32[128,128]{1,0:T(8,128)S(1)} %get-tuple-element.16), channel_id=1, source_target_pairs={{0,16},{4,20},{8,24},{12,28},{16,0},{20,4},{24,8},{28,12},{1,17},{... | collective-permute-start | bytes 196616 | tf_op jit(solution)/shard_map/ppermute | solution.py:344
  41.6 1.4 collective-permute-start.6
  42.9 0.2 collective-permute-start.4
  43.2 9.9 %merged.5.refs_0_ = f32[4096,2048]{1,0:T(8,128)} custom-call(f32[4096,2048]{1,0:T(8,128)} %merged.4.refs_0_, bf16[1024,4096]{1,0:T(8,128)(2,1)} %bitcast.83, bf16[4096,2048]{1,0:T(8,128)(2,1)} %bitcast.75, bf16[1024,2048]{1,0:T(8,128)(2,1)} %bitcast.90), custom_call_target="tpu_custom_call", output_to_operand_aliasing={{}: (0, {})} | custom-call | flops 4294967296 | bytes 18874368 | tf_op jit(solution)/shard_map/merged/pallas_call | solution.py:136
  53.1 3.0 %collective-permute-start.9 = (f32[128,128]{1,0:T(8,128)S(1)}, f32[128,128]{1,0:T(8,128)S(1)}, u32[]{:S(2)}, u32[]{:S(2)}) collective-permute-start(f32[128,128]{1,0:T(8,128)S(1)} %fusion.2), channel_id=1, source_target_pairs={{0,24},{4,28},{8,16},{12,20},{16,8},{20,12},{24,0},{28,4},{1,25},{... | collective-permute-start | bytes 196616 | tf_op jit(solution)/shard_map/ppermute | solution.py:344
  56.1 0.3 collective-permute-start.8
  56.4 1.1 collective-permute-start.7
  57.5 9.9 %merged.6.refs_0_ = f32[4096,2048]{1,0:T(8,128)} custom-call(f32[4096,2048]{1,0:T(8,128)} %merged.5.refs_0_, bf16[1024,4096]{1,0:T(8,128)(2,1)} %bitcast.84, bf16[4096,2048]{1,0:T(8,128)(2,1)} %bitcast.76, bf16[1024,2048]{1,0:T(8,128)(2,1)} %bitcast.91), custom_call_target="tpu_custom_call", output_to_operand_aliasing={{}: (0, {})} | custom-call | flops 4294967296 | bytes 18874368 | tf_op jit(solution)/shard_map/merged/pallas_call | solution.py:136
  67.5 1.6 collective-permute-start.13
  69.1 1.5 collective-permute-start.11
  70.6 9.9 %merged.7.refs_10_ = f32[4096,2048]{1,0:T(8,128)} custom-call(f32[4096,2048]{1,0:T(8,128)} %merged.6.refs_0_, bf16[1024,4096]{1,0:T(8,128)(2,1)} %bitcast.85, bf16[4096,2048]{1,0:T(8,128)(2,1)} %bitcast.77, bf16[1024,2048]{1,0:T(8,128)(2,1)} %bitcast.92), custom_call_target="tpu_custom_call", output_to_operand_aliasing={{}: (0, {})} | custom-call | flops 4294967296 | bytes 18874368 | tf_op jit(solution)/shard_map/merged/pallas_call | solution.py:136
  80.5 0.5 collective-permute-start.15
  81.1 6.7 %collective-permute-done.15.refs_3_ = f32[4,128,128]{2,1,0:T(8,128)S(1)} collective-permute-done((f32[4,128,128]{2,1,0:T(8,128)S(1)}, f32[4,128,128]{2,1,0:T(8,128)S(1)}, u32[]{:S(2)}, u32[]{:S(2)}) %collective-permute-start.15) | collective-permute-done | bytes 262176 | tf_op jit(solution)/shard_map/ppermute | solution.py:347
  87.9 0.5 collective-permute-start.14
  88.5 8.0 %right_terms.2 = (f32[1024,128]{1,0:T(8,128)S(1)}, f32[128,2048]{1,0:T(8,128)S(1)}) custom-call(s32[3]{0:T(128)S(1)} %pad_add_fusion.ids_ref, f32[4,128,128]{2,1,0:T(8,128)S(1)} %pad_maximum_fusion.refs_0_, f32[4,128,128]{2,1,0:T(8,128)S(1)} %collective-permute-done.11.refs_1_, f32[4,128,128]{2,1,0:T(8,128)S(1)} %collective-permute-done.13.refs_2_, ...), custom_call_target="tpu_custom_call" | custom-call | flops 3221225472 | bytes 12582912 | tf_op jit(solution)/shard_map/right_terms/pallas_call | solution.py:221
  96.5 10.6 %right_terms.3 = f32[128,2048]{1,0:T(8,128)S(1)} custom-call(s32[3]{0:T(128)S(1)} %pad_add_fusion.ids_ref, f32[4,128,128]{2,1,0:T(8,128)S(1)} %collective-permute-done.10.refs_0_.refs_4_, f32[4,128,128]{2,1,0:T(8,128)S(1)} %collective-permute-done.12.refs_1_.refs_5_, f32[4,128,128]{2,1,0:T(8,128)S(1)} %collective-permute-done.14.refs_2_.refs_6_, ...), custom_call_target="tpu_custom_call" | custom-call | flops 3221225472 | bytes 12582912 | tf_op jit(solution)/shard_map/right_terms/pallas_call | solution.py:221
  107.1 0.8 dynamic-slice_bitcast_fusion
  107.9 0.4 collective-permute-start.17
  108.4 3.6 %fusion.6 = f32[128,128]{1,0:T(8,128)S(1)} fusion(f32[4096,128]{1,0:T(8,128)S(1)} %constant_dynamic-update-slice_fusion), kind=kOutput, calls=%fused_computation.36 | convolution fusion | flops 805306368 | bytes 2162688 | tf_op jit(solution)/shard_map/dot_general | solution.py:380
  112.1 11.7 %cholesky.17 = f32[128,128]{1,0:T(8,128)S(1)} custom-call(f32[128,128]{1,0:T(8,128)S(1)} %fusion.5), custom_call_target="Cholesky" | custom-call | tf_op jit(solution)/shard_map/jit(cholesky)/cholesky | solution.py:381
  123.9 1.1 bitcast_add_fusion
  125.0 2.0 %collective-permute-start.19 = (f32[16,2048]{1,0:T(8,128)S(1)}, f32[16,2048]{1,0:T(8,128)S(1)}, u32[]{:S(2)}, u32[]{:S(2)}) collective-permute-start(f32[16,2048]{1,0:T(8,128)S(1)} %get-tuple-element.13), channel_id=1, source_target_pairs={{0,16},{4,20},{8,24},{12,28},{16,0},{20,4},{24,8},{28,12},{1,17},{... | collective-permute-start | bytes 393224 | tf_op jit(solution)/shard_map/ppermute | solution.py:344
  127.0 1.3 collective-permute-start.20
  128.3 0.2 collective-permute-start.18
  128.6 0.6 compare_reduce_fusion
  129.3 8.3 %collective-permute-done.19 = f32[16,2048]{1,0:T(8,128)S(1)} collective-permute-done((f32[16,2048]{1,0:T(8,128)S(1)}, f32[16,2048]{1,0:T(8,128)S(1)}, u32[]{:S(2)}, u32[]{:S(2)}) %collective-permute-start.19) | collective-permute-done | bytes 131104 | tf_op jit(solution)/shard_map/ppermute | solution.py:344
  137.5 0.9 collective-permute-done.18
  138.5 2.8 %collective-permute-start.23 = (f32[16,2048]{1,0:T(8,128)S(1)}, f32[16,2048]{1,0:T(8,128)S(1)}, u32[]{:S(2)}, u32[]{:S(2)}) collective-permute-start(f32[16,2048]{1,0:T(8,128)S(1)} %bitcast_add_fusion.1.refs_0_), channel_id=1, source_target_pairs={{0,24},{4,28},{8,16},{12,20},{16,8},{20,12},{24,0},{28,4},{1,25},{... | collective-permute-start | bytes 393224 | tf_op jit(solution)/shard_map/ppermute | solution.py:344
  141.4 0.7 collective-permute-start.22
  142.1 0.9 collective-permute-start.21
  143.0 0.7 fusion.1
  143.6 9.8 %custom-call.6 = f32[1,128,128]{1,2,0:T(8,128)S(1)} custom-call(f32[1,128,128]{2,1,0:T(8,128)S(1)} %fusion.1), custom_call_target="InvertDiagBlocksLowerTriangular" | custom-call | tf_op jit(solution)/shard_map/triangular_solve | solution.py:382
  153.5 0.5 collective-permute-start.27
  154.1 0.4 collective-permute-start.25
  154.5 0.2 fusion.3.refs_8_
  154.8 6.5 %left_factor.1.refs_9_ = bf16[4096,256]{1,0:T(8,128)(2,1)} custom-call(s32[3]{0:T(128)S(1)} %pad_add_fusion.ids_ref, f32[4,128,128]{2,1,0:T(8,128)S(1)} %pad_maximum_fusion.refs_0_, f32[4,128,128]{2,1,0:T(8,128)S(1)} %collective-permute-done.11.refs_1_, f32[4,128,128]{2,1,0:T(8,128)S(1)} %collective-permute-done.13.refs_2_, ...), custom_call_target="tpu_custom_call" | custom-call | flops 805306368 | bytes 4194304 | tf_op jit(solution)/shard_map/left_factor/pallas_call | solution.py:260
  161.3 1.6 copy-done
  162.9 23.1 %new_error.1 = (bf16[1,4096,2048]{2,1,0:T(8,128)(2,1)}, f32[2048,128]{1,0:T(8,128)}) custom-call(s32[3]{0:T(128)S(1)} %pad_add_fusion.ids_ref, f32[16,2048]{1,0:T(8,128)S(1)} %bitcast_add_fusion.1.refs_0_, f32[16,2048]{1,0:T(8,128)S(1)} %collective-permute-done.21.refs_1_, f32[16,2048]{1,0:T(8,128)S(1)} %collective-permute-done.22.refs_2_, ...), custom_call_target="tpu_custom_call" | custom-call | flops 8589934592 | bytes 50331648 | tf_op jit(solution)/shard_map/new_error/pallas_call | solution.py:306
  (51 shorter events, 1.2 us)
Async XLA Ops:
  0.6 1.2 copy-start.1
  13.7 8.2 %collective-permute-start = (f32[4,4,128,128]{3,2,1,0:T(8,128)S(1)}, f32[4,4,128,128]{3,2,1,0:T(8,128)S(1)}, u32[]{:S(2)}, u32[]{:S(2)}) collective-permute-start(f32[4,4,128,128]{3,2,1,0:T(8,128)S(1)} %left_terms.3), channel_id=1, source_target_pairs={{0,4},{4,0},{8,12},{12,8},{16,20},{20,16},{24,28},{28,24},{1,5},{5... | collective-permute-start | bytes 3145736 | tf_op jit(solution)/shard_map/ppermute | solution.py:341
  22.2 15.2 %collective-permute-start.2 = (f32[4,128,128]{2,1,0:T(8,128)S(1)}, f32[4,128,128]{2,1,0:T(8,128)S(1)}, u32[]{:S(2)}, u32[]{:S(2)}) collective-permute-start(f32[4,128,128]{2,1,0:T(8,128)S(1)} %get-tuple-element.10), channel_id=1, source_target_pairs={{0,2},{1,3},{2,0},{3,1},{4,6},{5,7},{6,4},{7,5},{8,10},{9,11},{10,... | collective-permute-start | bytes 786440 | tf_op jit(solution)/shard_map/ppermute | solution.py:347
  24.8 12.6 %collective-permute-start.3 = (f32[4,128,128]{2,1,0:T(8,128)S(1)}, f32[4,128,128]{2,1,0:T(8,128)S(1)}, u32[]{:S(2)}, u32[]{:S(2)}) collective-permute-start(f32[4,128,128]{2,1,0:T(8,128)S(1)} %get-tuple-element.11), channel_id=1, source_target_pairs={{0,3},{1,2},{2,1},{3,0},{4,7},{5,6},{6,5},{7,4},{8,11},{9,10},{10,... | collective-permute-start | bytes 786440 | tf_op jit(solution)/shard_map/ppermute | solution.py:347
  26.3 12.4 %collective-permute-start.1 = (f32[4,128,128]{2,1,0:T(8,128)S(1)}, f32[4,128,128]{2,1,0:T(8,128)S(1)}, u32[]{:S(2)}, u32[]{:S(2)}) collective-permute-start(f32[4,128,128]{2,1,0:T(8,128)S(1)} %get-tuple-element.12), channel_id=1, source_target_pairs={{0,1},{1,0},{2,3},{3,2},{4,5},{5,4},{6,7},{7,6},{8,9},{9,8},{10,11... | collective-permute-start | bytes 786440 | tf_op jit(solution)/shard_map/ppermute | solution.py:347
  38.8 14.3 %collective-permute-start.5 = (f32[128,128]{1,0:T(8,128)S(1)}, f32[128,128]{1,0:T(8,128)S(1)}, u32[]{:S(2)}, u32[]{:S(2)}) collective-permute-start(f32[128,128]{1,0:T(8,128)S(1)} %get-tuple-element.16), channel_id=1, source_target_pairs={{0,16},{4,20},{8,24},{12,28},{16,0},{20,4},{24,8},{28,12},{1,17},{... | collective-permute-start | bytes 196616 | tf_op jit(solution)/shard_map/ppermute | solution.py:344
  41.6 11.5 %collective-permute-start.6 = (f32[128,128]{1,0:T(8,128)S(1)}, f32[128,128]{1,0:T(8,128)S(1)}, u32[]{:S(2)}, u32[]{:S(2)}) collective-permute-start(f32[128,128]{1,0:T(8,128)S(1)} %get-tuple-element.17), channel_id=1, source_target_pairs={{0,24},{4,28},{8,16},{12,20},{16,8},{20,12},{24,0},{28,4},{1,25},{... | collective-permute-start | bytes 196616 | tf_op jit(solution)/shard_map/ppermute | solution.py:344
  42.9 10.1 %collective-permute-start.4 = (f32[128,128]{1,0:T(8,128)S(1)}, f32[128,128]{1,0:T(8,128)S(1)}, u32[]{:S(2)}, u32[]{:S(2)}) collective-permute-start(f32[128,128]{1,0:T(8,128)S(1)} %get-tuple-element.18), channel_id=1, source_target_pairs={{0,8},{4,12},{8,0},{12,4},{16,24},{20,28},{24,16},{28,20},{1,9},{5... | collective-permute-start | bytes 196616 | tf_op jit(solution)/shard_map/ppermute | solution.py:344
  53.1 14.4 %collective-permute-start.9 = (f32[128,128]{1,0:T(8,128)S(1)}, f32[128,128]{1,0:T(8,128)S(1)}, u32[]{:S(2)}, u32[]{:S(2)}) collective-permute-start(f32[128,128]{1,0:T(8,128)S(1)} %fusion.2), channel_id=1, source_target_pairs={{0,24},{4,28},{8,16},{12,20},{16,8},{20,12},{24,0},{28,4},{1,25},{... | collective-permute-start | bytes 196616 | tf_op jit(solution)/shard_map/ppermute | solution.py:344
  56.1 11.4 %collective-permute-start.8 = (f32[128,128]{1,0:T(8,128)S(1)}, f32[128,128]{1,0:T(8,128)S(1)}, u32[]{:S(2)}, u32[]{:S(2)}) collective-permute-start(f32[128,128]{1,0:T(8,128)S(1)} %fusion.2), channel_id=1, source_target_pairs={{0,16},{4,20},{8,24},{12,28},{16,0},{20,4},{24,8},{28,12},{1,17},{... | collective-permute-start | bytes 196616 | tf_op jit(solution)/shard_map/ppermute | solution.py:344
  56.4 11.1 %collective-permute-start.7 = (f32[128,128]{1,0:T(8,128)S(1)}, f32[128,128]{1,0:T(8,128)S(1)}, u32[]{:S(2)}, u32[]{:S(2)}) collective-permute-start(f32[128,128]{1,0:T(8,128)S(1)} %fusion.2), channel_id=1, source_target_pairs={{0,8},{4,12},{8,0},{12,4},{16,24},{20,28},{24,16},{28,20},{1,9},{5... | collective-permute-start | bytes 196616 | tf_op jit(solution)/shard_map/ppermute | solution.py:344
  67.5 13.5 %collective-permute-start.13 = (f32[4,128,128]{2,1,0:T(8,128)S(1)}, f32[4,128,128]{2,1,0:T(8,128)S(1)}, u32[]{:S(2)}, u32[]{:S(2)}) collective-permute-start(f32[4,128,128]{2,1,0:T(8,128)S(1)} %pad_maximum_fusion.refs_0_), channel_id=1, source_target_pairs={{0,2},{1,3},{2,0},{3,1},{4,6},{5,7},{6,4},{7,5},{8,10},{9,11},{10,... | collective-permute-start | bytes 786440 | tf_op jit(solution)/shard_map/ppermute | solution.py:347
  69.1 11.9 %collective-permute-start.11 = (f32[4,128,128]{2,1,0:T(8,128)S(1)}, f32[4,128,128]{2,1,0:T(8,128)S(1)}, u32[]{:S(2)}, u32[]{:S(2)}) collective-permute-start(f32[4,128,128]{2,1,0:T(8,128)S(1)} %pad_maximum_fusion.refs_0_), channel_id=1, source_target_pairs={{0,1},{1,0},{2,3},{3,2},{4,5},{5,4},{6,7},{7,6},{8,9},{9,8},{10,11... | collective-permute-start | bytes 786440 | tf_op jit(solution)/shard_map/ppermute | solution.py:347
  80.5 7.3 %collective-permute-start.15 = (f32[4,128,128]{2,1,0:T(8,128)S(1)}, f32[4,128,128]{2,1,0:T(8,128)S(1)}, u32[]{:S(2)}, u32[]{:S(2)}) collective-permute-start(f32[4,128,128]{2,1,0:T(8,128)S(1)} %pad_maximum_fusion.refs_0_), channel_id=1, source_target_pairs={{0,3},{1,2},{2,1},{3,0},{4,7},{5,6},{6,5},{7,4},{8,11},{9,10},{10,... | collective-permute-start | bytes 786440 | tf_op jit(solution)/shard_map/ppermute | solution.py:347
  81.0 6.8 %collective-permute-start.10 = (f32[4,128,128]{2,1,0:T(8,128)S(1)}, f32[4,128,128]{2,1,0:T(8,128)S(1)}, u32[]{:S(2)}, u32[]{:S(2)}) collective-permute-start(f32[4,128,128]{2,1,0:T(8,128)S(1)} %pad_maximum_fusion.refs_0_), channel_id=1, source_target_pairs={{0,4},{4,0},{8,12},{12,8},{16,20},{20,16},{24,28},{28,24},{1,5},{5... | collective-permute-start | bytes 786440 | tf_op jit(solution)/shard_map/ppermute | solution.py:341
  87.8 8.6 %collective-permute-start.16 = (f32[4,128,128]{2,1,0:T(8,128)S(1)}, f32[4,128,128]{2,1,0:T(8,128)S(1)}, u32[]{:S(2)}, u32[]{:S(2)}) collective-permute-start(f32[4,128,128]{2,1,0:T(8,128)S(1)} %collective-permute-done.15.refs_3_), channel_id=1, source_target_pairs={{0,4},{4,0},{8,12},{12,8},{16,20},{20,16},{24,28},{28,24},{1,5},{5... | collective-permute-start | bytes 786440 | tf_op jit(solution)/shard_map/ppermute | solution.py:341
  87.9 8.6 %collective-permute-start.14 = (f32[4,128,128]{2,1,0:T(8,128)S(1)}, f32[4,128,128]{2,1,0:T(8,128)S(1)}, u32[]{:S(2)}, u32[]{:S(2)}) collective-permute-start(f32[4,128,128]{2,1,0:T(8,128)S(1)} %collective-permute-done.13.refs_2_), channel_id=1, source_target_pairs={{0,4},{4,0},{8,12},{12,8},{16,20},{20,16},{24,28},{28,24},{1,5},{5... | collective-permute-start | bytes 786440 | tf_op jit(solution)/shard_map/ppermute | solution.py:341
  88.4 8.1 %collective-permute-start.12 = (f32[4,128,128]{2,1,0:T(8,128)S(1)}, f32[4,128,128]{2,1,0:T(8,128)S(1)}, u32[]{:S(2)}, u32[]{:S(2)}) collective-permute-start(f32[4,128,128]{2,1,0:T(8,128)S(1)} %collective-permute-done.11.refs_1_), channel_id=1, source_target_pairs={{0,4},{4,0},{8,12},{12,8},{16,20},{20,16},{24,28},{28,24},{1,5},{5... | collective-permute-start | bytes 786440 | tf_op jit(solution)/shard_map/ppermute | solution.py:341
  107.9 15.9 %collective-permute-start.17 = (f32[4,16,2048]{2,1,0:T(8,128)}, f32[4,16,2048]{2,1,0:T(8,128)}, u32[]{:S(2)}, u32[]{:S(2)}) collective-permute-start(f32[4,16,2048]{2,1,0:T(8,128)} %dynamic-slice_bitcast_fusion), channel_id=1, source_target_pairs={{0,4},{4,0},{8,12},{12,8},{16,20},{20,16},{24,28},{28,24},{1,5},{5... | collective-permute-start | bytes 1572872 | tf_op jit(solution)/shard_map/ppermute | solution.py:341
  125.0 12.5 %collective-permute-start.19 = (f32[16,2048]{1,0:T(8,128)S(1)}, f32[16,2048]{1,0:T(8,128)S(1)}, u32[]{:S(2)}, u32[]{:S(2)}) collective-permute-start(f32[16,2048]{1,0:T(8,128)S(1)} %get-tuple-element.13), channel_id=1, source_target_pairs={{0,16},{4,20},{8,24},{12,28},{16,0},{20,4},{24,8},{28,12},{1,17},{... | collective-permute-start | bytes 393224 | tf_op jit(solution)/shard_map/ppermute | solution.py:344
  127.0 10.5 %collective-permute-start.20 = (f32[16,2048]{1,0:T(8,128)S(1)}, f32[16,2048]{1,0:T(8,128)S(1)}, u32[]{:S(2)}, u32[]{:S(2)}) collective-permute-start(f32[16,2048]{1,0:T(8,128)S(1)} %get-tuple-element.14), channel_id=1, source_target_pairs={{0,24},{4,28},{8,16},{12,20},{16,8},{20,12},{24,0},{28,4},{1,25},{... | collective-permute-start | bytes 393224 | tf_op jit(solution)/shard_map/ppermute | solution.py:344
  128.3 10.1 %collective-permute-start.18 = (f32[16,2048]{1,0:T(8,128)S(1)}, f32[16,2048]{1,0:T(8,128)S(1)}, u32[]{:S(2)}, u32[]{:S(2)}) collective-permute-start(f32[16,2048]{1,0:T(8,128)S(1)} %get-tuple-element.15), channel_id=1, source_target_pairs={{0,8},{4,12},{8,0},{12,4},{16,24},{20,28},{24,16},{28,20},{1,9},{5... | collective-permute-start | bytes 393224 | tf_op jit(solution)/shard_map/ppermute | solution.py:344
  138.5 15.0 %collective-permute-start.23 = (f32[16,2048]{1,0:T(8,128)S(1)}, f32[16,2048]{1,0:T(8,128)S(1)}, u32[]{:S(2)}, u32[]{:S(2)}) collective-permute-start(f32[16,2048]{1,0:T(8,128)S(1)} %bitcast_add_fusion.1.refs_0_), channel_id=1, source_target_pairs={{0,24},{4,28},{8,16},{12,20},{16,8},{20,12},{24,0},{28,4},{1,25},{... | collective-permute-start | bytes 393224 | tf_op jit(solution)/shard_map/ppermute | solution.py:344
  141.4 12.7 %collective-permute-start.22 = (f32[16,2048]{1,0:T(8,128)S(1)}, f32[16,2048]{1,0:T(8,128)S(1)}, u32[]{:S(2)}, u32[]{:S(2)}) collective-permute-start(f32[16,2048]{1,0:T(8,128)S(1)} %bitcast_add_fusion.1.refs_0_), channel_id=1, source_target_pairs={{0,16},{4,20},{8,24},{12,28},{16,0},{20,4},{24,8},{28,12},{1,17},{... | collective-permute-start | bytes 393224 | tf_op jit(solution)/shard_map/ppermute | solution.py:344
  142.1 12.1 %collective-permute-start.21 = (f32[16,2048]{1,0:T(8,128)S(1)}, f32[16,2048]{1,0:T(8,128)S(1)}, u32[]{:S(2)}, u32[]{:S(2)}) collective-permute-start(f32[16,2048]{1,0:T(8,128)S(1)} %bitcast_add_fusion.1.refs_0_), channel_id=1, source_target_pairs={{0,8},{4,12},{8,0},{12,4},{16,24},{20,28},{24,16},{28,20},{1,9},{5... | collective-permute-start | bytes 393224 | tf_op jit(solution)/shard_map/ppermute | solution.py:344
  153.4 7.9 %collective-permute-start.24 = (f32[16,2048]{1,0:T(8,128)S(1)}, f32[16,2048]{1,0:T(8,128)S(1)}, u32[]{:S(2)}, u32[]{:S(2)}) collective-permute-start(f32[16,2048]{1,0:T(8,128)S(1)} %bitcast_add_fusion.1.refs_0_), channel_id=1, source_target_pairs={{0,4},{4,0},{8,12},{12,8},{16,20},{20,16},{24,28},{28,24},{1,5},{5... | collective-permute-start | bytes 393224 | tf_op jit(solution)/shard_map/ppermute | solution.py:341
  153.5 7.8 %collective-permute-start.27 = (f32[16,2048]{1,0:T(8,128)S(1)}, f32[16,2048]{1,0:T(8,128)S(1)}, u32[]{:S(2)}, u32[]{:S(2)}) collective-permute-start(f32[16,2048]{1,0:T(8,128)S(1)} %collective-permute-done.23.refs_3_), channel_id=1, source_target_pairs={{0,4},{4,0},{8,12},{12,8},{16,20},{20,16},{24,28},{28,24},{1,5},{5... | collective-permute-start | bytes 393224 | tf_op jit(solution)/shard_map/ppermute | solution.py:341
  154.0 7.3 %collective-permute-start.26 = (f32[16,2048]{1,0:T(8,128)S(1)}, f32[16,2048]{1,0:T(8,128)S(1)}, u32[]{:S(2)}, u32[]{:S(2)}) collective-permute-start(f32[16,2048]{1,0:T(8,128)S(1)} %collective-permute-done.22.refs_2_), channel_id=1, source_target_pairs={{0,4},{4,0},{8,12},{12,8},{16,20},{20,16},{24,28},{28,24},{1,5},{5... | collective-permute-start | bytes 393224 | tf_op jit(solution)/shard_map/ppermute | solution.py:341
  154.1 7.2 %collective-permute-start.25 = (f32[16,2048]{1,0:T(8,128)S(1)}, f32[16,2048]{1,0:T(8,128)S(1)}, u32[]{:S(2)}, u32[]{:S(2)}) collective-permute-start(f32[16,2048]{1,0:T(8,128)S(1)} %collective-permute-done.21.refs_1_), channel_id=1, source_target_pairs={{0,4},{4,0},{8,12},{12,8},{16,20},{20,16},{24,28},{28,24},{1,5},{5... | collective-permute-start | bytes 393224 | tf_op jit(solution)/shard_map/ppermute | solution.py:341
  161.3 1.6 copy-start

commit v2 on v0

v2 whole, which is shorter than its diff:
```python
import functools

import jax
import jax.numpy as jnp
from jax import lax
from jax.experimental import pallas as pl
from jax.experimental.pallas import tpu as pltpu
from jax.sharding import PartitionSpec as P

F32 = jnp.float32
BF16 = jnp.bfloat16
HIGHEST = lax.Precision.HIGHEST
RANK = 128
VMEM_LIMIT = 50 * 1024 * 1024
SMALL_LIMIT = 6 * 1024 * 1024
MERGED_LIMIT = 8 * 1024 * 1024
RIGHT_LIMIT = 11 * 1024 * 1024
FINAL_LIMIT = 9 * 1024 * 1024


def params(limit=VMEM_LIMIT):
    return pltpu.CompilerParams(vmem_limit_bytes=limit)


def cost(flops, nbytes):
    return pl.CostEstimate(flops=flops, bytes_accessed=nbytes, transcendentals=0)


def split_rows(x):
    hi = x.astype(BF16)
    lo = (x - hi.astype(F32)).astype(BF16)
    return jnp.concatenate([hi, lo], axis=0)


def fold(y):
    return y[:RANK] + y[RANK:]


def dot(a, b, contract=((1,), (0,))):
    return lax.dot_general(a, b, (contract, ((), ())), preferred_element_type=F32)


ROWS_BY_ROWS = ((1,), (1,))


def skipping(count, body, *refs):
    body(*refs[count:])


def in_vmem(body, outs, args, name, limit=SMALL_LIMIT, work=None, after=()):
    args = [*after, *args]
    return pl.pallas_call(
        functools.partial(skipping, len(after), body),
        in_specs=[pl.BlockSpec(memory_space=pl.ANY)] * len(after)
        + [pl.BlockSpec(memory_space=pltpu.VMEM)] * (len(args) - len(after)),
        out_specs=[pl.BlockSpec(memory_space=pltpu.VMEM)] * len(outs),
        out_shape=[jax.ShapeDtypeStruct(*out) for out in outs],
        compiler_params=params(limit),
        cost_estimate=work,
        name=name,
    )(*args)


def u_kernel(g_ref, q_ref, ucat_ref, qcat_ref):
    @pl.when(pl.program_id(0) == 0)
    def _():
        qcat_ref[...] = split_rows(q_ref[...].T)

    ucat_ref[...] = split_rows(fold(dot(qcat_ref[...], g_ref[...], ROWS_BY_ROWS)))


def grads_by_q(g, q):
    tok, cols = g.shape
    tile = tok // 2
    return pl.pallas_call(
        u_kernel,
        grid=(tok // tile,),
        in_specs=[
            pl.BlockSpec((tile, cols), lambda i: (i, 0)),
            pl.BlockSpec((cols, RANK), lambda i: (0, 0)),
        ],
        out_specs=[
            pl.BlockSpec((2 * RANK, tile), lambda i: (0, i)),
            pl.BlockSpec((2 * RANK, cols), lambda i: (0, 0)),
        ],
        out_shape=[
            jax.ShapeDtypeStruct((2 * RANK, tok), BF16),
            jax.ShapeDtypeStruct((2 * RANK, cols), BF16),
        ],
        compiler_params=params(),
        cost_estimate=cost(4 * tok * cols * RANK, tok * cols * 2 + cols * RANK * 8),
        name="grads_by_q",
    )(g, q)


def p_kernel(nz, ids_ref, a_ref, e_ref, ucat_ref, qcat_ref, p_ref, acc_ref):
    acc = dot(qcat_ref[...], e_ref[...], ROWS_BY_ROWS) + dot(ucat_ref[...], a_ref[...])
    acc_ref[...] = fold(acc).T
    rows = p_ref.shape[2]
    for k in range(nz):
        start = pl.multiple_of((ids_ref[2] ^ k) * rows, rows)
        p_ref[0, k] = acc_ref[pl.ds(start, rows), :]


def left_terms(ids, a, e, ucat, qcat, kc, nm, nz):
    tok, rows = a.shape
    cols = e.shape[1]
    tile = rows // (2 * nm)

    def block(j, ids_ref):
        return (ids_ref[0] ^ kc) * nm + (ids_ref[1] ^ j)

    return pl.pallas_call(
        functools.partial(p_kernel, nz),
        grid_spec=pltpu.PrefetchScalarGridSpec(
            num_scalar_prefetch=1,
            grid=(nm,),
            in_specs=[
                pl.BlockSpec((tok, tile), lambda j, ids_ref: (0, block(j, ids_ref))),
                pl.BlockSpec((tile, cols), lambda j, ids_ref: (block(j, ids_ref), 0)),
                pl.BlockSpec((2 * RANK, tok), lambda j, ids_ref: (0, 0)),
                pl.BlockSpec((2 * RANK, cols), lambda j, ids_ref: (0, 0)),
            ],
            out_specs=pl.BlockSpec((1, nz, tile // nz, RANK), lambda j, ids_ref: (j, 0, 0, 0)),
            scratch_shapes=[pltpu.VMEM((tile, RANK), F32)],
        ),
        out_shape=jax.ShapeDtypeStruct((nm, nz, tile // nz, RANK), F32),
        compiler_params=params(),
        cost_estimate=cost(2 * rows * RANK * (tok + cols), rows * (tok + cols)),
        name="left_terms",
    )(ids, a, e, ucat, qcat)


def first_sum_kernel(keeps, sends, near_ref, far_ref, *outs):
    rows = near_ref.shape[2] // 2
    for half in range(2):
        for out, members in ((outs[2 * half], sends[half]), (outs[2 * half + 1], keeps[half])):
            for i, km in enumerate(members):
                at = (km, slice(None), pl.ds(half * rows, rows))
                out[i] = near_ref[at] + far_ref[at]


def next_sum_kernel(keeps, sends, *refs):
    ins, outs = refs[:4], refs[4:]
    for half in range(2):
        kept, came = ins[2 * half : 2 * half + 2]
        for out, places in ((outs[2 * half], sends[half]), (outs[2 * half + 1], keeps[half])):
            for i, at in enumerate(places):
                out[i] = kept[at] + came[at]


def last_sum_kernel(nz, *refs):
    ins, outs = refs[:4], refs[4:]
    rows = ins[0].shape[2]
    for k in range(nz):
        for half in range(2):
            outs[k][pl.ds(half * rows, rows), :] = ins[2 * half][0, k] + ins[2 * half + 1][0, k]


def scatter_over_mp(near, far, to_mp, orders, beside):
    nm, nz, block, _ = near.shape
    rows = block // 2
    members = [list(range(nm))] * 2
    values, done = None, ()
    for step in range(len(orders[0])):
        bits = [1 << order[step] for order in orders]
        keep_lists = [[km for km in members[h] if not km & bits[h]] for h in range(2)]
        send_lists = [[km | bits[h] for km in keep_lists[h]] for h in range(2)]
        count = len(keep_lists[0])
        outs = [((count, nz, rows, RANK), F32)] * 4
        if values is None:
            parts = in_vmem(functools.partial(first_sum_kernel, keep_lists, send_lists), outs, [near, far], "first_sum")
        else:
            keep_at = [[members[h].index(km) for km in keep_lists[h]] for h in range(2)]
            send_at = [[members[h].index(km) for km in send_lists[h]] for h in range(2)]
            parts = in_vmem(functools.partial(next_sum_kernel, keep_at, send_at), outs, values, "next_sum", after=done)
            done = ()
        members = keep_lists
        came = [to_mp(parts[0], bits[0]), to_mp(parts[2], bits[1])]
        if step == 0:
            done = [beside(parts[1])]
        values = [parts[1], came[0], parts[3], came[1]]
    return in_vmem(functools.partial(last_sum_kernel, nz), [((block, RANK), F32)] * nz, values, "last_sum", after=done)


def own_sum_kernel(*refs):
    ins, out = refs[:-1], refs[-1]
    total = ins[0][...]
    for came in ins[1:]:
        total = total + came[...]
    out[...] = total


def own_kernel(nz, *refs):
    ins, outs = refs[:nz], refs[nz:]
    rows = outs[0].shape[2]
    for k in range(nz):
        for half in range(2):
            outs[half][0, k] = ins[k][pl.ds(half * rows, rows), :]


def grow_kernel(*refs):
    ins, outs = refs[:4], refs[4:]
    count = ins[0].shape[0]
    for half in range(2):
        outs[half][pl.ds(0, count)] = ins[2 * half][...]
        outs[half][pl.ds(count, count)] = ins[2 * half + 1][...]


def gather_over_mp(pieces, to_mp, orders, done):
    nz = len(pieces)
    rows = pieces[0].shape[0] // 2
    held = in_vmem(functools.partial(own_kernel, nz), [((1, nz, rows, RANK), F32)] * 2, pieces, "own_rows", after=done)
    members = [[0], [0]]
    last = len(orders[0]) - 1
    for step in range(last, -1, -1):
        bits = [1 << order[step] for order in orders]
        came = [to_mp(held[h], bits[h]) for h in range(2)]
        came_members = [[km ^ bits[h] for km in members[h]] for h in range(2)]
        if step == 0:
            return [held[0], held[1], came[0], came[1]], [
                (0, members[0]), (1, members[1]), (0, came_members[0]), (1, came_members[1])
            ]
        count = len(members[0])
        held = in_vmem(
            grow_kernel, [((2 * count, nz, rows, RANK), F32)] * 2, [held[0], came[0], held[1], came[1]], "grow"
        )
        members = [members[h] + came_members[h] for h in range(2)]


def merged_kernel(part, after_ref, a_ref, e_ref, g_ref, out_ref):
    tok, cols = g_ref.shape
    rows = out_ref.shape[0]
    tile = rows // 4

    def body(a_tile, e_tile):
        start = pl.multiple_of(pl.program_id(0) * tile, tile)
        out_ref[pl.ds(start, tile), :] = dot(a_tile[...], g_ref[...], ((0,), (0,))) + e_tile[...].astype(F32)

    pltpu.emit_pipeline(
        body,
        grid=(4,),
        in_specs=[
            pl.BlockSpec((tok, tile), lambda i: (0, part * 4 + i)),
            pl.BlockSpec((tile, cols), lambda i: (part * 4 + i, 0)),
        ],
    )(a_ref, e_ref)


def merged_part(a, e, g, part, parts, after):
    tok, rows = a.shape
    cols = e.shape[1]
    return pl.pallas_call(
        functools.partial(merged_kernel, part),
        in_specs=[pl.BlockSpec(memory_space=pl.ANY)]
        + [pl.BlockSpec(memory_space=pltpu.HBM)] * 2
        + [pl.BlockSpec(memory_space=pltpu.VMEM)],
        out_specs=pl.BlockSpec(memory_space=pltpu.VMEM),
        out_shape=pltpu.VMEM((rows // parts, cols), F32),
        compiler_params=params(MERGED_LIMIT),
        cost_estimate=cost(2 * tok * cols * rows // parts, (rows * cols * 2 + rows * tok * 2) // parts),
        name="merged",
    )(after, a, e, g)


def q_kernel(owners, kc, nm, nz, last, ids_ref, *refs):
    pieces, refs = refs[:4], refs[4:]
    if last:
        v_in, q_in, gram_in, a_ref, e_ref, g_ref, send_ref, keep_ref, gram_ref, p_half, v_acc, q_acc, gram_acc = refs
        v_acc[...], q_acc[...], gram_acc[...] = v_in[...], q_in[...], gram_in[...]
    else:
        a_ref, e_ref, v_acc, q_acc, gram_acc, p_half = refs
        for acc in (v_acc, q_acc, gram_acc):
            acc[...] = jnp.zeros_like(acc)
    rows = pieces[0].shape[2]
    tok, cols = a_ref.shape[0], e_ref.shape[1]
    tile = p_half.shape[0] // nm
    for piece, (half, members) in zip(pieces, owners):
        for i, km in enumerate(members):
            for k in range(nz):
                start = ((ids_ref[1] ^ km) * nz + (ids_ref[2] ^ k)) * (2 * rows) + half * rows
                p_half[pl.ds(pl.multiple_of(start, rows), rows), :] = piece[i, k]
    first = (ids_ref[0] ^ kc) * nm

    def body(a_tile, e_tile):
        start = pl.multiple_of(pl.program_id(0) * tile, tile)
        pcat = split_rows(p_half[pl.ds(start, tile), :].T)
        v_acc[...] += fold(dot(pcat, a_tile[...], ROWS_BY_ROWS))
        q_acc[...] += fold(dot(pcat, e_tile[...]))
        gram_acc[...] += dot(pcat, pcat, ROWS_BY_ROWS)

    pltpu.emit_pipeline(
        body,
        grid=(nm,),
        in_specs=[
            pl.BlockSpec((tok, tile), lambda j: (0, first + j)),
            pl.BlockSpec((tile, cols), lambda j: (first + j, 0)),
        ],
    )(a_ref, e_ref)

    if last:
        q_acc[...] += fold(dot(split_rows(v_acc[...]), g_ref[...]))
        whole = fold(gram_acc[...])
        gram_ref[...] = whole[:, :RANK] + whole[:, RANK:]
        small = send_ref.shape[1]
        for out, flip in ((send_ref, 1), (keep_ref, 0)):
            for k in range(nz):
                start = ((ids_ref[0] ^ flip) * nz + (ids_ref[2] ^ k)) * small
                out[k] = q_acc[pl.ds(pl.multiple_of(start, small), small), :]


def right_terms(ids, pieces, owners, a, e, g, kc, nm, before=None):
    tok, rows = a.shape
    cols = e.shape[1]
    nz = pieces[0].shape[1]
    last = before is not None
    vmem = pl.BlockSpec(memory_space=pltpu.VMEM)
    hbm = pl.BlockSpec(memory_space=pltpu.HBM)
    sums = [(RANK, tok), (RANK, cols), (2 * RANK, 2 * RANK)]
    scratch = [pltpu.VMEM((rows // 2, RANK), F32)]
    if last:
        specs = [vmem] * 7 + [hbm] * 2 + [vmem]
        args = [*pieces, *before, a, e, g]
        outs = [(nz, RANK // (2 * nz), cols)] * 2 + [(RANK, RANK)]
        scratch += [pltpu.VMEM(shape, F32) for shape in sums]
    else:
        specs = [vmem] * 4 + [hbm] * 2
        args = [*pieces, a, e]
        outs = sums
    return pl.pallas_call(
        functools.partial(q_kernel, owners, kc, nm, nz, last),
        grid_spec=pltpu.PrefetchScalarGridSpec(
            num_scalar_prefetch=1,
            grid=(),
            in_specs=specs,
            out_specs=[vmem] * 3,
            scratch_shapes=scratch,
        ),
        out_shape=[jax.ShapeDtypeStruct(shape, F32) for shape in outs],
        compiler_params=params(RIGHT_LIMIT),
        cost_estimate=cost(2 * rows * RANK * (tok + cols), rows * (tok + cols)),
        name="right_terms",
    )(ids, *args)


def chol_inverse_kernel(gram_ref, out_ref):
    left = gram_ref[...]
    row = lax.broadcasted_iota(jnp.int32, (RANK, RANK), 0)
    right = (row == lax.broadcasted_iota(jnp.int32, (RANK, RANK), 1)).astype(F32)
    for j in range(RANK):
        at = j % 8
        if j and at == 0:
            left, right = left[8:], right[8:]
        pivot_row, own = left[at : at + 1], right[at : at + 1]
        pivot = pivot_row[:, j : j + 1]
        out_ref[j : j + 1, :] = own * (1.0 / jnp.sqrt(pivot))
        inverse = 1.0 / pivot
        below = row[: left.shape[0], :1] > at
        factor = jnp.where(below, left[:, j : j + 1], 0.0)
        left = left - factor * (pivot_row * inverse)
        right = right - factor * (own * inverse)


def p_hat_kernel(owners, nm, nz, ids_ref, after_ref, *refs):
    pieces, (inv_ref, out_ref, p_all) = refs[:8], refs[8:]
    rows = pieces[0].shape[2]
    for h in range(2):
        for piece, (half, members) in zip(pieces[4 * h : 4 * h + 4], owners):
            for i, km in enumerate(members):
                for k in range(nz):
                    block = ((ids_ref[0] ^ h) * nm + (ids_ref[1] ^ km)) * nz + (ids_ref[2] ^ k)
                    start = block * (2 * rows) + half * rows
                    p_all[pl.ds(pl.multiple_of(start, rows), rows), :] = piece[i, k]
    inv_hi = inv_ref[...].T.astype(BF16)
    inv_lo = (inv_ref[...].T - inv_hi.astype(F32)).astype(BF16)
    inv = jnp.concatenate([inv_hi, inv_hi, inv_lo, inv_lo], axis=0)
    tile = p_all.shape[0] // 8

    @pl.loop(0, 8)
    def _(i):
        at = pl.ds(pl.multiple_of(i * tile, tile), tile)
        x = p_all[at, :]
        hi = x.astype(BF16)
        lo = (x - hi.astype(F32)).astype(BF16)
        y = dot(jnp.concatenate([hi, lo, hi, lo], axis=1), inv)
        y_hi = y.astype(BF16)
        y_lo = (y - y_hi.astype(F32)).astype(BF16)
        out_ref[at, :] = jnp.concatenate([y_hi, y_lo], axis=1)


def left_factor(ids, pieces, owners, inv, rows, nm, nz, after):
    return pl.pallas_call(
        functools.partial(p_hat_kernel, owners, nm, nz),
        grid_spec=pltpu.PrefetchScalarGridSpec(
            num_scalar_prefetch=1,
            grid=(),
            in_specs=[pl.BlockSpec(memory_space=pl.ANY)] + [pl.BlockSpec(memory_space=pltpu.VMEM)] * 9,
            out_specs=pl.BlockSpec(memory_space=pltpu.VMEM),
            scratch_shapes=[pltpu.VMEM((rows, RANK), F32)],
        ),
        out_shape=jax.ShapeDtypeStruct((rows, 2 * RANK), BF16),
        compiler_params=params(SMALL_LIMIT),
        cost_estimate=cost(8 * rows * RANK * RANK, rows * RANK * 8),
        name="left_factor",
    )(ids, after, *pieces, inv)


def final_kernel(nz, scale, tile, ids_ref, *refs):
    pieces, refs = refs[: 2 * nz], refs[2 * nz :]
    inv_ref, phat_ref, parts, (err_ref, qnew_ref, q_sum, q_cat) = refs[0], refs[1], refs[2:6], refs[6:]
    small = pieces[0].shape[0]
    for h in range(2):
        for k in range(nz):
            block = (ids_ref[0] ^ h) * nz + (ids_ref[2] ^ k)
            q_sum[pl.ds(pl.multiple_of(block * small, small), small), :] = pieces[h * nz + k][...]
    q_t = scale * lax.dot_general(
        inv_ref[...], q_sum[...], (((1,), (0,)), ((), ())), precision=HIGHEST, preferred_element_type=F32
    )
    qnew_ref[...] = q_t.T
    hi = q_t.astype(BF16)
    lo = (q_t - hi.astype(F32)).astype(BF16)
    q_cat[...] = jnp.concatenate([hi, hi, lo, lo], axis=0)
    part_rows, cols = parts[0].shape
    steps = part_rows // tile
    for number, merged in enumerate(parts):

        def body(out_tile):
            start = pl.multiple_of(pl.program_id(0) * tile, tile)
            x = phat_ref[pl.ds(pl.multiple_of(number * part_rows + start, tile), tile), :]
            approx = dot(jnp.concatenate([x, x], axis=1), q_cat[...])
            out_tile[0] = (merged[pl.ds(start, tile), :] - approx).astype(BF16)

        pltpu.emit_pipeline(
            body,
            grid=(steps,),
            in_specs=[],
            out_specs=[pl.BlockSpec((1, tile, cols), lambda i, number=number: (0, number * steps + i, 0))],
        )(err_ref)


def finish(ids, pieces, inv, phat, parts, replicas):
    nz = len(pieces) // 2
    part_rows, cols = parts[0].shape
    rows = part_rows * len(parts)
    vmem = pl.BlockSpec(memory_space=pltpu.VMEM)
    hbm = pl.BlockSpec(memory_space=pltpu.HBM)
    return pl.pallas_call(
        functools.partial(final_kernel, nz, 1.0 / replicas, rows // 16),
        grid_spec=pltpu.PrefetchScalarGridSpec(
            num_scalar_prefetch=1,
            grid=(),
            in_specs=[vmem] * (2 * nz + 1) + [vmem] + [vmem] * len(parts),
            out_specs=[hbm, vmem],
            scratch_shapes=[pltpu.VMEM((RANK, cols), F32), pltpu.VMEM((4 * RANK, cols), BF16)],
        ),
        out_shape=[jax.ShapeDtypeStruct((1, rows, cols), BF16), jax.ShapeDtypeStruct((cols, RANK), F32)],
        compiler_params=params(FINAL_LIMIT),
        cost_estimate=cost(8 * rows * cols * RANK, rows * cols * 6),
        name="new_error",
    )(ids, *pieces, inv, phat, *parts)


def q_sum_kernel(nz, *refs):
    keep, came, outs = refs[0], refs[1], refs[2:]
    for k in range(nz):
        outs[k][...] = keep[k] + came[k]


def per_device(n_dp, n_mp, activations, out_grads, error_fb, q_prev):
    a, g, e = activations[0], out_grads[0], error_fb[0]
    a_hbm = pltpu.with_memory_space_constraint(a, pltpu.HBM)
    e_hbm = pltpu.with_memory_space_constraint(e, pltpu.HBM)
    rows = a.shape[1]
    nz = n_dp // 2
    dp, mp = lax.axis_index("dp"), lax.axis_index("mp")
    ids = jnp.stack([dp % 2, mp, dp // 2]).astype(jnp.int32)
    bits = list(range(n_mp.bit_length() - 1))
    orders = [bits, bits[::-1]]

    def to_core(x):
        return lax.ppermute(x, "dp", [(i, i ^ 1) for i in range(n_dp)])

    def to_z(x, k):
        return lax.ppermute(x, "dp", [(i, i ^ (2 * k)) for i in range(n_dp)])

    def to_mp(x, k):
        return lax.ppermute(x, "mp", [(i, i ^ k) for i in range(n_mp)])

    ucat, qcat = grads_by_q(g, q_prev)
    p_far = left_terms(ids, a, e, ucat, qcat, 1, n_mp, nz)
    p_arrived = to_core(p_far)
    p_near = left_terms(ids, a, e, ucat, qcat, 0, n_mp, nz)
    parts = []

    def beside(sent):
        parts.append(merged_part(a_hbm, e_hbm, g, len(parts), 4, sent))
        return parts[-1]

    by_z = scatter_over_mp(p_near, p_arrived, to_mp, orders, beside)
    done = [beside(by_z[0])]
    came = [to_z(by_z[k], k) for k in range(1, nz)]
    [p_own] = in_vmem(own_sum_kernel, [(by_z[0].shape, F32)], [by_z[0], *came], "p_own", after=done)
    done = [beside(p_own)]
    p_pieces = [p_own] + [to_z(p_own, k) for k in range(1, nz)]
    near, owners = gather_over_mp(p_pieces, to_mp, orders, done)
    beside(near[0])
    far = [to_core(x) for x in near]

    half = right_terms(ids, near, owners, a_hbm, e_hbm, g, 0, n_mp)
    q_send, q_keep, gram = right_terms(ids, far, owners, a_hbm, e_hbm, g, 1, n_mp, half)

    piece = (q_keep.shape[1:], F32)
    q_by_z = in_vmem(functools.partial(q_sum_kernel, nz), [piece] * nz, [q_keep, to_core(q_send)], "q_sum")
    q_own = q_by_z[0] + sum(to_z(q_by_z[k], k) for k in range(1, nz))
    q_near = [q_own] + [to_z(q_own, k) for k in range(1, nz)]
    q_pieces = q_near + [to_core(x) for x in q_near]

    square = ((RANK, RANK), F32)
    [inv] = in_vmem(chol_inverse_kernel, [square], [gram], "chol_inverse", work=cost(2 * 10**10, 10**5))
    phat = left_factor(ids, near + far, owners, inv, rows, n_mp, nz, q_own)
    new_error, q_new = finish(ids, q_pieces, inv, phat, parts, n_dp)
    return new_error, q_new


def solution(mesh):
    placed = (P("dp", None, None), P("dp", None, "mp"), P("dp", None, "mp"), P("mp", None))
    return jax.shard_map(
        functools.partial(per_device, mesh.shape["dp"], mesh.shape["mp"]),
        mesh=mesh,
        in_specs=placed,
        out_specs=(P("dp", None, "mp"), P("mp", None)),
        check_vma=False,
    )
```

time: 397 us -> 164 us (0.41); the launches traced: 392 us -> 163 us
  waiting for transfers between devices: 194 us -> 28.8 us
  matrix products: 159 us -> 0 us
  Pallas kernels: 0 us -> 98.9 us
  starting transfers between devices: 0.48 us -> 29.8 us
  other arithmetic: 24.2 us -> 0.11 us
  between operations: 14.3 us -> 1.02 us
  local copies, waits for them, and re-layouts: 0.11 us -> 4.63 us
    psum x2 -> x0, waiting for transfers between devices: 194 us -> none  [the longest x1 136 us: per_device(): p_sum = lax.psum(p_local, ('dp', 'mp'))]
    dot_general x5 -> x0, matrix products: 156 us -> none  [the longest x1 57 us: per_device(): lax.dot_general(merged, p_hat, (((0,), (0,)), ((), ())), precision=lax.Pr...]
    pallas_call x0 -> x19, Pallas kernels: none -> 98.9 us  [the longest x4 27.9 us: merged_part(): pl.pallas_call(functools.partial(merged_kernel, part), in_specs=[pl.Block...]
    ppermute x0 -> x30, starting transfers between devices: none -> 29.8 us  [the longest x12 17.8 us: to_z(): return lax.ppermute(x, 'dp', [(i, i ^ 2 * k) for i in range(n_dp)])]
    ppermute x0 -> x30, waiting for transfers between devices: none -> 28.8 us  [the longest x8 15.5 us: to_mp(): return lax.ppermute(x, 'mp', [(i, i ^ k) for i in range(n_mp)])]
    another operation x5 -> x1, other arithmetic: 22.9 us -> 0.08 us  [per_device(): ids = jnp.stack([dp % 2, mp, dp // 2]).astype(jnp.int32)]
    unnamed x6 -> x16, local copies, waits for them, and re-layouts: 0.02 us -> 4.63 us
  transfers between devices with their start and end apart: 2 -> 30, of which waited for: 2 -> 10; matrix products, arithmetic and copies ran while one was open for 0% -> 0% of each run, Pallas kernels for 0% -> 36%
where the time goes in v2:
time: 164 us; the launch traced here: 163 us
  Pallas kernels  98.9 us (60%)
  starting transfers between devices  29.8 us (18%)
  waiting for transfers between devices  28.8 us (18%)
  local copies, waits for them, and re-layouts  4.63 us (3%)
    pallas_call x4, Pallas kernels, merged_part(): pl.pallas_call(functools.partial(merged_kernel, part), in_specs=[pl.Block...  27.9 us
    pallas_call x1, Pallas kernels, finish(): pl.pallas_call(functools.partial(final_kernel, nz, 1.0 / replicas, rows /...  19.3 us
    ppermute x12, starting transfers between devices, to_z(): return lax.ppermute(x, 'dp', [(i, i ^ 2 * k) for i in range(n_dp)])  17.8 us
    pallas_call x2, Pallas kernels, right_terms(): pl.pallas_call(functools.partial(q_kernel, owners, kc, nm, nz, last), gri...  17.8 us
    pallas_call x2, Pallas kernels, left_terms(): pl.pallas_call(functools.partial(p_kernel, nz), grid_spec=pltpu.PrefetchS...  16.1 us
    ppermute x8, waiting for transfers between devices, to_mp(): return lax.ppermute(x, 'mp', [(i, i ^ k) for i in range(n_mp)])  15.5 us
    ppermute x12, waiting for transfers between devices, to_z(): return lax.ppermute(x, 'dp', [(i, i ^ 2 * k) for i in range(n_dp)])  11.7 us
    pallas_call x8, Pallas kernels, in_vmem(): pl.pallas_call(functools.partial(skipping, len(after), body), in_specs=[p...  11.1 us
  transfers between devices with their start and end apart: 30, of which 10 were waited for; matrix products, arithmetic and copies ran while one was open for 0% of the time, Pallas kernels for 36%

profile of v2, /device:TPU:0, one launch (start us, length us, event | category | flops | bytes accessed | tf_op | source)
XLA Modules:
  0.0 163.3 jit_solution(5697226570081539074)
XLA Ops:
  0.7 1.2 copy-done.3
  1.9 3.5 %grads_by_q.1 = (bf16[256,1024]{1,0:T(8,128)(2,1)S(1)}, bf16[256,2048]{1,0:T(8,128)(2,1)S(1)}) custom-call(bf16[1024,2048]{1,0:T(8,128)(2,1)} %bitcast.6, f32[2048,128]{1,0:T(8,128)S(1)} %copy-done.3), custom_call_target="tpu_custom_call" | custom-call | flops 1073741824 | bytes 6291456 | tf_op jit(solution)/shard_map/grads_by_q/pallas_call | solution.py:75
  5.5 8.0 %left_terms.3 = f32[4,4,128,128]{3,2,1,0:T(8,128)S(1)} custom-call(s32[3]{0:T(128)S(1)} %pad_add_fusion.ids_ref, bf16[1024,4096]{1,0:T(8,128)(2,1)} %bitcast.24, bf16[4096,2048]{1,0:T(8,128)(2,1)} %bitcast.16, bf16[256,1024]{1,0:T(8,128)(2,1)S(1)} %get-tuple-element.30.ucat_ref, bf16[256,2048]{1,0:T(8,128)(2,1)S(1)} %get-tuple-element.31.qcat_ref), custom_call_target="tpu_custom_call" | custom-call | flops 3221225472 | bytes 12582912 | tf_op jit(solution)/shard_map/left_terms/pallas_call | solution.py:113
  13.4 0.5 collective-permute-start
  13.9 8.1 %left_terms.2.refs_0_ = f32[4,4,128,128]{3,2,1,0:T(8,128)S(1)} custom-call(s32[3]{0:T(128)S(1)} %pad_add_fusion.ids_ref, bf16[1024,4096]{1,0:T(8,128)(2,1)} %bitcast.25, bf16[4096,2048]{1,0:T(8,128)(2,1)} %bitcast.17, bf16[256,1024]{1,0:T(8,128)(2,1)S(1)} %get-tuple-element.30.ucat_ref, bf16[256,2048]{1,0:T(8,128)(2,1)S(1)} %get-tuple-element.31.qcat_ref), custom_call_target="tpu_custom_call" | custom-call | flops 3221225472 | bytes 12582912 | tf_op jit(solution)/shard_map/left_terms/pallas_call | solution.py:113
  22.1 0.2 first_sum.1
  22.2 2.7 %collective-permute-start.1 = (f32[2,4,64,128]{3,2,1,0:T(8,128)S(1)}, f32[2,4,64,128]{3,2,1,0:T(8,128)S(1)}, u32[]{:S(2)}, u32[]{:S(2)}) collective-permute-start(f32[2,4,64,128]{3,2,1,0:T(8,128)S(1)} %get-tuple-element.33), channel_id=1, source_target_pairs={{0,1},{1,0},{2,3},{3,2},{4,5},{5,4},{6,7},{7,6},{8,9},{9,8},{10,11... | collective-permute-start | bytes 786440 | tf_op jit(solution)/shard_map/ppermute | solution.py:487
  24.9 1.5 collective-permute-start.2
  26.4 6.8 %merged.4.refs_0_.refs_10_ = f32[1024,2048]{1,0:T(8,128)S(1)} custom-call(f32[2,4,64,128]{3,2,1,0:T(8,128)S(1)} %get-tuple-element.32.after_ref.refs_1_, bf16[1024,4096]{1,0:T(8,128)(2,1)} %bitcast.26, bf16[4096,2048]{1,0:T(8,128)(2,1)} %bitcast.18, bf16[1024,2048]{1,0:T(8,128)(2,1)S(1)} %bitcast.7), custom_call_target="tpu_custom_call" | custom-call | flops 4294967296 | bytes 6291456 | tf_op jit(solution)/shard_map/merged/pallas_call | solution.py:253
  33.3 1.4 collective-permute-start.3
  34.7 0.6 collective-permute-start.4
  35.2 3.2 %collective-permute-done.3.refs_1_ = f32[1,4,64,128]{3,2,1,0:T(8,128)S(1)} collective-permute-done((f32[1,4,64,128]{3,2,1,0:T(8,128)S(1)}, f32[1,4,64,128]{3,2,1,0:T(8,128)S(1)}, u32[]{:S(2)}, u32[]{:S(2)}) %collective-permute-start.3) | collective-permute-done | bytes 131104 | tf_op jit(solution)/shard_map/ppermute | solution.py:487
  38.4 1.3 collective-permute-done.4.refs_3_
  39.7 1.7 %collective-permute-start.5 = (f32[128,128]{1,0:T(8,128)S(1)}, f32[128,128]{1,0:T(8,128)S(1)}, u32[]{:S(2)}, u32[]{:S(2)}) collective-permute-start(f32[128,128]{1,0:T(8,128)S(1)} %get-tuple-element.41), channel_id=1, source_target_pairs={{0,8},{4,12},{8,0},{12,4},{16,24},{20,28},{24,16},{28,20},{1,9},{5... | collective-permute-start | bytes 196616 | tf_op jit(solution)/shard_map/ppermute | solution.py:484
  41.4 2.6 %collective-permute-start.6 = (f32[128,128]{1,0:T(8,128)S(1)}, f32[128,128]{1,0:T(8,128)S(1)}, u32[]{:S(2)}, u32[]{:S(2)}) collective-permute-start(f32[128,128]{1,0:T(8,128)S(1)} %get-tuple-element.42), channel_id=1, source_target_pairs={{0,16},{4,20},{8,24},{12,28},{16,0},{20,4},{24,8},{28,12},{1,17},{... | collective-permute-start | bytes 196616 | tf_op jit(solution)/shard_map/ppermute | solution.py:484
  43.9 0.2 collective-permute-start.7
  44.2 6.8 %merged.5.refs_0_.refs_11_ = f32[1024,2048]{1,0:T(8,128)S(1)} custom-call(f32[128,128]{1,0:T(8,128)S(1)} %get-tuple-element.40.after_ref.refs_1_, bf16[1024,4096]{1,0:T(8,128)(2,1)} %bitcast.27, bf16[4096,2048]{1,0:T(8,128)(2,1)} %bitcast.19, bf16[1024,2048]{1,0:T(8,128)(2,1)S(1)} %bitcast.8), custom_call_target="tpu_custom_call" | custom-call | flops 4294967296 | bytes 6291456 | tf_op jit(solution)/shard_map/merged/pallas_call | solution.py:253
  51.0 3.4 %copy-done.1 = f32[1024,2048]{1,0:T(8,128)} copy-done((f32[1024,2048]{1,0:T(8,128)}, f32[1024,2048]{1,0:T(8,128)S(1)}, u32[]{:S(2)}) %copy-start.1) | copy-done | bytes 8388632
  54.4 3.6 %collective-permute-start.10 = (f32[128,128]{1,0:T(8,128)S(1)}, f32[128,128]{1,0:T(8,128)S(1)}, u32[]{:S(2)}, u32[]{:S(2)}) collective-permute-start(f32[128,128]{1,0:T(8,128)S(1)} %p_own.1.after_ref.refs_1_), channel_id=1, source_target_pairs={{0,24},{4,28},{8,16},{12,20},{16,8},{20,12},{24,0},{28,4},{1,25},{... | collective-permute-start | bytes 196616 | tf_op jit(solution)/shard_map/ppermute | solution.py:484
  58.0 0.8 collective-permute-start.8
  58.8 6.8 %merged.6.refs_0_.refs_12_ = f32[1024,2048]{1,0:T(8,128)S(1)} custom-call(f32[128,128]{1,0:T(8,128)S(1)} %p_own.1.after_ref.refs_1_, bf16[1024,4096]{1,0:T(8,128)(2,1)} %bitcast.28, bf16[4096,2048]{1,0:T(8,128)(2,1)} %bitcast.20, bf16[1024,2048]{1,0:T(8,128)(2,1)S(1)} %bitcast.9), custom_call_target="tpu_custom_call" | custom-call | flops 4294967296 | bytes 6291456 | tf_op jit(solution)/shard_map/merged/pallas_call | solution.py:253
  65.6 0.8 collective-permute-start.11
  66.4 0.6 collective-permute-start.12
  66.9 4.9 %collective-permute-done.11.refs_1_ = f32[1,4,64,128]{3,2,1,0:T(8,128)S(1)} collective-permute-done((f32[1,4,64,128]{3,2,1,0:T(8,128)S(1)}, f32[1,4,64,128]{3,2,1,0:T(8,128)S(1)}, u32[]{:S(2)}, u32[]{:S(2)}) %collective-permute-start.11) | collective-permute-done | bytes 131104 | tf_op jit(solution)/shard_map/ppermute | solution.py:487
  71.8 0.9 collective-permute-done.12.refs_3_
  72.8 1.4 collective-permute-start.17
  74.2 0.5 collective-permute-start.15
  74.7 0.5 collective-permute-start.13
  75.2 4.0 %collective-permute-done.17.refs_3_ = f32[2,4,64,128]{3,2,1,0:T(8,128)S(1)} collective-permute-done((f32[2,4,64,128]{3,2,1,0:T(8,128)S(1)}, f32[2,4,64,128]{3,2,1,0:T(8,128)S(1)}, u32[]{:S(2)}, u32[]{:S(2)}) %collective-permute-start.17) | collective-permute-done | bytes 262176 | tf_op jit(solution)/shard_map/ppermute | solution.py:487
  79.2 1.4 collective-permute-done.15.refs_2_
  80.6 8.2 %right_terms.2 = (f32[128,1024]{1,0:T(8,128)S(1)}, f32[128,2048]{1,0:T(8,128)S(1)}, f32[256,256]{1,0:T(8,128)S(1)}) custom-call(s32[3]{0:T(128)S(1)} %pad_add_fusion.ids_ref, f32[2,4,64,128]{3,2,1,0:T(8,128)S(1)} %get-tuple-element.46.refs_0_.after_ref, f32[2,4,64,128]{3,2,1,0:T(8,128)S(1)} %get-tuple-element.47.refs_1_, ...), custom_call_target="tpu_custom_call" | custom-call | flops 3221225472 | bytes 12582912 | tf_op jit(solution)/shard_map/right_terms/pallas_call | solution.py:330
  88.8 9.5 %right_terms.3 = (f32[4,16,2048]{2,1,0:T(8,128)S(1)}, f32[4,16,2048]{2,1,0:T(8,128)S(1)}, f32[128,128]{1,0:T(8,128)S(1)}) custom-call(s32[3]{0:T(128)S(1)} %pad_add_fusion.ids_ref, f32[2,4,64,128]{3,2,1,0:T(8,128)S(1)} %collective-permute-done.13.refs_0_.refs_4_, f32[2,4,64,128]{3,2,1,0:T(8,128)S(1)} %collective-permute-done.14.refs_1_.refs_5_, ...), custom_call_target="tpu_custom_call" | custom-call | flops 3221225472 | bytes 12582912 | tf_op jit(solution)/shard_map/right_terms/pallas_call | solution.py:330
  98.4 0.6 collective-permute-start.19
  98.9 1.5 collective-permute-done.19.refs_1_
  100.5 1.2 collective-permute-start.20
  101.7 3.1 %collective-permute-start.21 = (f32[16,2048]{1,0:T(8,128)S(1)}, f32[16,2048]{1,0:T(8,128)S(1)}, u32[]{:S(2)}, u32[]{:S(2)}) collective-permute-start(f32[16,2048]{1,0:T(8,128)S(1)} %get-tuple-element.55), channel_id=1, source_target_pairs={{0,16},{4,20},{8,24},{12,28},{16,0},{20,4},{24,8},{28,12},{1,17},{... | collective-permute-start | bytes 393224 | tf_op jit(solution)/shard_map/ppermute | solution.py:484
  104.8 0.2 collective-permute-start.22
  105.0 3.8 %collective-permute-done.20 = f32[16,2048]{1,0:T(8,128)S(1)} collective-permute-done((f32[16,2048]{1,0:T(8,128)S(1)}, f32[16,2048]{1,0:T(8,128)S(1)}, u32[]{:S(2)}, u32[]{:S(2)}) %collective-permute-start.20) | collective-permute-done | bytes 131104 | tf_op jit(solution)/shard_map/ppermute | solution.py:484
  108.8 6.0 %collective-permute-done.21 = f32[16,2048]{1,0:T(8,128)S(1)} collective-permute-done((f32[16,2048]{1,0:T(8,128)S(1)}, f32[16,2048]{1,0:T(8,128)S(1)}, u32[]{:S(2)}, u32[]{:S(2)}) %collective-permute-start.21) | collective-permute-done | bytes 131104 | tf_op jit(solution)/shard_map/ppermute | solution.py:484
  114.8 2.5 %collective-permute-start.25 = (f32[16,2048]{1,0:T(8,128)S(1)}, f32[16,2048]{1,0:T(8,128)S(1)}, u32[]{:S(2)}, u32[]{:S(2)}) collective-permute-start(f32[16,2048]{1,0:T(8,128)S(1)} %add_add_fusion.after_ref.refs_0_), channel_id=1, source_target_pairs={{0,24},{4,28},{8,16},{12,20},{16,8},{20,12},{24,0},{28,4},{1,25},{... | collective-permute-start | bytes 393224 | tf_op jit(solution)/shard_map/ppermute | solution.py:484
  117.3 1.8 %collective-permute-start.24 = (f32[16,2048]{1,0:T(8,128)S(1)}, f32[16,2048]{1,0:T(8,128)S(1)}, u32[]{:S(2)}, u32[]{:S(2)}) collective-permute-start(f32[16,2048]{1,0:T(8,128)S(1)} %add_add_fusion.after_ref.refs_0_), channel_id=1, source_target_pairs={{0,16},{4,20},{8,24},{12,28},{16,0},{20,4},{24,8},{28,12},{1,17},{... | collective-permute-start | bytes 393224 | tf_op jit(solution)/shard_map/ppermute | solution.py:484
  119.3 7.6 %merged.7.refs_13_ = f32[1024,2048]{1,0:T(8,128)S(1)} custom-call(f32[2,4,64,128]{3,2,1,0:T(8,128)S(1)} %get-tuple-element.46.refs_0_.after_ref, bf16[1024,4096]{1,0:T(8,128)(2,1)} %bitcast.31, bf16[4096,2048]{1,0:T(8,128)(2,1)} %bitcast.23, bf16[1024,2048]{1,0:T(8,128)(2,1)S(1)} %bitcast.11), custom_call_target="tpu_custom_call" | custom-call | flops 4294967296 | bytes 6291456 | tf_op jit(solution)/shard_map/merged/pallas_call | solution.py:253
  127.0 0.5 collective-permute-start.29
  127.5 2.0 %collective-permute-done.24.refs_2_ = f32[16,2048]{1,0:T(8,128)S(1)} collective-permute-done((f32[16,2048]{1,0:T(8,128)S(1)}, f32[16,2048]{1,0:T(8,128)S(1)}, u32[]{:S(2)}, u32[]{:S(2)}) %collective-permute-start.24) | collective-permute-done | bytes 131104 | tf_op jit(solution)/shard_map/ppermute | solution.py:484
  129.5 0.5 collective-permute-start.27
  130.0 10.7 %chol_inverse.1.refs_8_ = f32[128,128]{1,0:T(8,128)S(1)} custom-call(f32[128,128]{1,0:T(8,128)S(1)} %get-tuple-element.57.refs_0_), custom_call_target="tpu_custom_call" | custom-call | flops 20000000000 | bytes 100000 | tf_op jit(solution)/shard_map/chol_inverse/pallas_call | solution.py:52
  140.7 3.2 %left_factor.1.refs_9_ = bf16[4096,256]{1,0:T(8,128)(2,1)S(1)} custom-call(s32[3]{0:T(128)S(1)} %pad_add_fusion.ids_ref, f32[16,2048]{1,0:T(8,128)S(1)} %add_add_fusion.after_ref.refs_0_, f32[2,4,64,128]{3,2,1,0:T(8,128)S(1)} %get-tuple-element.46.refs_0_.after_ref, f32[2,4,64,128]{3,2,1,0:T(8,128)S(1)} %get-tuple-element.47.refs_1_, ...), custom_call_target="tpu_custom_call" | custom-call | flops 536870912 | bytes 4194304 | tf_op jit(solution)/shard_map/left_factor/pallas_call | solution.py:392
  144.0 19.3 %new_error.1 = (bf16[1,4096,2048]{2,1,0:T(8,128)(2,1)}, f32[2048,128]{1,0:T(8,128)}) custom-call(s32[3]{0:T(128)S(1)} %pad_add_fusion.ids_ref, f32[16,2048]{1,0:T(8,128)S(1)} %add_add_fusion.after_ref.refs_0_, f32[16,2048]{1,0:T(8,128)S(1)} %collective-permute-done.23.refs_1_, f32[16,2048]{1,0:T(8,128)S(1)} %collective-permute-done.24.refs_2_, ...), custom_call_target="tpu_custom_call" | custom-call | flops 8589934592 | bytes 50331648 | tf_op jit(solution)/shard_map/new_error/pallas_call | solution.py:447
  (51 shorter events, 0.6 us)
Async XLA Ops:
  0.7 1.2 copy-start.3
  13.4 13.0 %copy-start = (bf16[1,1024,2048]{2,1,0:T(8,128)(2,1)S(1)}, bf16[1,1024,2048]{2,1,0:T(8,128)(2,1)}, u32[]{:S(2)}) copy-start(bf16[1,1024,2048]{2,1,0:T(8,128)(2,1)} %param.5) | copy-start | bytes 12582916
  13.4 8.6 %collective-permute-start = (f32[4,4,128,128]{3,2,1,0:T(8,128)S(1)}, f32[4,4,128,128]{3,2,1,0:T(8,128)S(1)}, u32[]{:S(2)}, u32[]{:S(2)}) collective-permute-start(f32[4,4,128,128]{3,2,1,0:T(8,128)S(1)} %left_terms.3), channel_id=1, source_target_pairs={{0,4},{4,0},{8,12},{12,8},{16,20},{20,16},{24,28},{28,24},{1,5},{5... | collective-permute-start | bytes 3145736 | tf_op jit(solution)/shard_map/ppermute | solution.py:481
  22.2 11.0 %collective-permute-start.1 = (f32[2,4,64,128]{3,2,1,0:T(8,128)S(1)}, f32[2,4,64,128]{3,2,1,0:T(8,128)S(1)}, u32[]{:S(2)}, u32[]{:S(2)}) collective-permute-start(f32[2,4,64,128]{3,2,1,0:T(8,128)S(1)} %get-tuple-element.33), channel_id=1, source_target_pairs={{0,1},{1,0},{2,3},{3,2},{4,5},{5,4},{6,7},{7,6},{8,9},{9,8},{10,11... | collective-permute-start | bytes 786440 | tf_op jit(solution)/shard_map/ppermute | solution.py:487
  24.9 8.3 %collective-permute-start.2 = (f32[2,4,64,128]{3,2,1,0:T(8,128)S(1)}, f32[2,4,64,128]{3,2,1,0:T(8,128)S(1)}, u32[]{:S(2)}, u32[]{:S(2)}) collective-permute-start(f32[2,4,64,128]{3,2,1,0:T(8,128)S(1)} %get-tuple-element.35), channel_id=1, source_target_pairs={{0,2},{1,3},{2,0},{3,1},{4,6},{5,7},{6,4},{7,5},{8,10},{9,11},{10,... | collective-permute-start | bytes 786440 | tf_op jit(solution)/shard_map/ppermute | solution.py:487
  33.3 5.1 %collective-permute-start.3 = (f32[1,4,64,128]{3,2,1,0:T(8,128)S(1)}, f32[1,4,64,128]{3,2,1,0:T(8,128)S(1)}, u32[]{:S(2)}, u32[]{:S(2)}) collective-permute-start(f32[1,4,64,128]{3,2,1,0:T(8,128)S(1)} %get-tuple-element.37), channel_id=1, source_target_pairs={{0,2},{1,3},{2,0},{3,1},{4,6},{5,7},{6,4},{7,5},{8,10},{9,11},{10,... | collective-permute-start | bytes 393224 | tf_op jit(solution)/shard_map/ppermute | solution.py:487
  34.7 5.0 %collective-permute-start.4 = (f32[1,4,64,128]{3,2,1,0:T(8,128)S(1)}, f32[1,4,64,128]{3,2,1,0:T(8,128)S(1)}, u32[]{:S(2)}, u32[]{:S(2)}) collective-permute-start(f32[1,4,64,128]{3,2,1,0:T(8,128)S(1)} %get-tuple-element.39), channel_id=1, source_target_pairs={{0,1},{1,0},{2,3},{3,2},{4,5},{5,4},{6,7},{7,6},{8,9},{9,8},{10,11... | collective-permute-start | bytes 393224 | tf_op jit(solution)/shard_map/ppermute | solution.py:487
  39.7 11.2 %collective-permute-start.5 = (f32[128,128]{1,0:T(8,128)S(1)}, f32[128,128]{1,0:T(8,128)S(1)}, u32[]{:S(2)}, u32[]{:S(2)}) collective-permute-start(f32[128,128]{1,0:T(8,128)S(1)} %get-tuple-element.41), channel_id=1, source_target_pairs={{0,8},{4,12},{8,0},{12,4},{16,24},{20,28},{24,16},{28,20},{1,9},{5... | collective-permute-start | bytes 196616 | tf_op jit(solution)/shard_map/ppermute | solution.py:484
  41.4 9.6 %collective-permute-start.6 = (f32[128,128]{1,0:T(8,128)S(1)}, f32[128,128]{1,0:T(8,128)S(1)}, u32[]{:S(2)}, u32[]{:S(2)}) collective-permute-start(f32[128,128]{1,0:T(8,128)S(1)} %get-tuple-element.42), channel_id=1, source_target_pairs={{0,16},{4,20},{8,24},{12,28},{16,0},{20,4},{24,8},{28,12},{1,17},{... | collective-permute-start | bytes 196616 | tf_op jit(solution)/shard_map/ppermute | solution.py:484
  43.9 7.0 %collective-permute-start.7 = (f32[128,128]{1,0:T(8,128)S(1)}, f32[128,128]{1,0:T(8,128)S(1)}, u32[]{:S(2)}, u32[]{:S(2)}) collective-permute-start(f32[128,128]{1,0:T(8,128)S(1)} %get-tuple-element.43), channel_id=1, source_target_pairs={{0,24},{4,28},{8,16},{12,20},{16,8},{20,12},{24,0},{28,4},{1,25},{... | collective-permute-start | bytes 196616 | tf_op jit(solution)/shard_map/ppermute | solution.py:484
  51.0 3.4 %copy-start.1 = (f32[1024,2048]{1,0:T(8,128)}, f32[1024,2048]{1,0:T(8,128)S(1)}, u32[]{:S(2)}) copy-start(f32[1024,2048]{1,0:T(8,128)S(1)} %merged.5.refs_0_.refs_11_) | copy-start | bytes 25165828
  54.4 11.2 %collective-permute-start.10 = (f32[128,128]{1,0:T(8,128)S(1)}, f32[128,128]{1,0:T(8,128)S(1)}, u32[]{:S(2)}, u32[]{:S(2)}) collective-permute-start(f32[128,128]{1,0:T(8,128)S(1)} %p_own.1.after_ref.refs_1_), channel_id=1, source_target_pairs={{0,24},{4,28},{8,16},{12,20},{16,8},{20,12},{24,0},{28,4},{1,25},{... | collective-permute-start | bytes 196616 | tf_op jit(solution)/shard_map/ppermute | solution.py:484
  58.0 7.6 %collective-permute-start.9 = (f32[128,128]{1,0:T(8,128)S(1)}, f32[128,128]{1,0:T(8,128)S(1)}, u32[]{:S(2)}, u32[]{:S(2)}) collective-permute-start(f32[128,128]{1,0:T(8,128)S(1)} %p_own.1.after_ref.refs_1_), channel_id=1, source_target_pairs={{0,16},{4,20},{8,24},{12,28},{16,0},{20,4},{24,8},{28,12},{1,17},{... | collective-permute-start | bytes 196616 | tf_op jit(solution)/shard_map/ppermute | solution.py:484
  58.0 7.6 %collective-permute-start.8 = (f32[128,128]{1,0:T(8,128)S(1)}, f32[128,128]{1,0:T(8,128)S(1)}, u32[]{:S(2)}, u32[]{:S(2)}) collective-permute-start(f32[128,128]{1,0:T(8,128)S(1)} %p_own.1.after_ref.refs_1_), channel_id=1, source_target_pairs={{0,8},{4,12},{8,0},{12,4},{16,24},{20,28},{24,16},{28,20},{1,9},{5... | collective-permute-start | bytes 196616 | tf_op jit(solution)/shard_map/ppermute | solution.py:484
  65.5 23.2 %copy-start.2 = (f32[1024,2048]{1,0:T(8,128)}, f32[1024,2048]{1,0:T(8,128)S(1)}, u32[]{:S(2)}) copy-start(f32[1024,2048]{1,0:T(8,128)S(1)} %merged.6.refs_0_.refs_12_) | copy-start | bytes 25165828
  65.6 6.2 %collective-permute-start.11 = (f32[1,4,64,128]{3,2,1,0:T(8,128)S(1)}, f32[1,4,64,128]{3,2,1,0:T(8,128)S(1)}, u32[]{:S(2)}, u32[]{:S(2)}) collective-permute-start(f32[1,4,64,128]{3,2,1,0:T(8,128)S(1)} %get-tuple-element.44.refs_0_), channel_id=1, source_target_pairs={{0,2},{1,3},{2,0},{3,1},{4,6},{5,7},{6,4},{7,5},{8,10},{9,11},{10,... | collective-permute-start | bytes 393224 | tf_op jit(solution)/shard_map/ppermute | solution.py:487
  66.4 6.4 %collective-permute-start.12 = (f32[1,4,64,128]{3,2,1,0:T(8,128)S(1)}, f32[1,4,64,128]{3,2,1,0:T(8,128)S(1)}, u32[]{:S(2)}, u32[]{:S(2)}) collective-permute-start(f32[1,4,64,128]{3,2,1,0:T(8,128)S(1)} %get-tuple-element.45.refs_2_), channel_id=1, source_target_pairs={{0,1},{1,0},{2,3},{3,2},{4,5},{5,4},{6,7},{7,6},{8,9},{9,8},{10,11... | collective-permute-start | bytes 393224 | tf_op jit(solution)/shard_map/ppermute | solution.py:487
  72.8 6.4 %collective-permute-start.17 = (f32[2,4,64,128]{3,2,1,0:T(8,128)S(1)}, f32[2,4,64,128]{3,2,1,0:T(8,128)S(1)}, u32[]{:S(2)}, u32[]{:S(2)}) collective-permute-start(f32[2,4,64,128]{3,2,1,0:T(8,128)S(1)} %get-tuple-element.47.refs_1_), channel_id=1, source_target_pairs={{0,2},{1,3},{2,0},{3,1},{4,6},{5,7},{6,4},{7,5},{8,10},{9,11},{10,... | collective-permute-start | bytes 786440 | tf_op jit(solution)/shard_map/ppermute | solution.py:487
  74.2 6.4 %collective-permute-start.15 = (f32[2,4,64,128]{3,2,1,0:T(8,128)S(1)}, f32[2,4,64,128]{3,2,1,0:T(8,128)S(1)}, u32[]{:S(2)}, u32[]{:S(2)}) collective-permute-start(f32[2,4,64,128]{3,2,1,0:T(8,128)S(1)} %get-tuple-element.46.refs_0_.after_ref), channel_id=1, source_target_pairs={{0,1},{1,0},{2,3},{3,2},{4,5},{5,4},{6,7},{7,6},{8,9},{9,8},{10,11... | collective-permute-start | bytes 786440 | tf_op jit(solution)/shard_map/ppermute | solution.py:487
  74.7 14.1 %collective-permute-start.14 = (f32[2,4,64,128]{3,2,1,0:T(8,128)S(1)}, f32[2,4,64,128]{3,2,1,0:T(8,128)S(1)}, u32[]{:S(2)}, u32[]{:S(2)}) collective-permute-start(f32[2,4,64,128]{3,2,1,0:T(8,128)S(1)} %get-tuple-element.47.refs_1_), channel_id=1, source_target_pairs={{0,4},{4,0},{8,12},{12,8},{16,20},{20,16},{24,28},{28,24},{1,5},{5... | collective-permute-start | bytes 786440 | tf_op jit(solution)/shard_map/ppermute | solution.py:481
  74.7 14.1 %collective-permute-start.13 = (f32[2,4,64,128]{3,2,1,0:T(8,128)S(1)}, f32[2,4,64,128]{3,2,1,0:T(8,128)S(1)}, u32[]{:S(2)}, u32[]{:S(2)}) collective-permute-start(f32[2,4,64,128]{3,2,1,0:T(8,128)S(1)} %get-tuple-element.46.refs_0_.after_ref), channel_id=1, source_target_pairs={{0,4},{4,0},{8,12},{12,8},{16,20},{20,16},{24,28},{28,24},{1,5},{5... | collective-permute-start | bytes 786440 | tf_op jit(solution)/shard_map/ppermute | solution.py:481
  79.2 9.6 %collective-permute-start.18 = (f32[2,4,64,128]{3,2,1,0:T(8,128)S(1)}, f32[2,4,64,128]{3,2,1,0:T(8,128)S(1)}, u32[]{:S(2)}, u32[]{:S(2)}) collective-permute-start(f32[2,4,64,128]{3,2,1,0:T(8,128)S(1)} %collective-permute-done.17.refs_3_), channel_id=1, source_target_pairs={{0,4},{4,0},{8,12},{12,8},{16,20},{20,16},{24,28},{28,24},{1,5},{5... | collective-permute-start | bytes 786440 | tf_op jit(solution)/shard_map/ppermute | solution.py:481
  80.6 8.3 %collective-permute-start.16 = (f32[2,4,64,128]{3,2,1,0:T(8,128)S(1)}, f32[2,4,64,128]{3,2,1,0:T(8,128)S(1)}, u32[]{:S(2)}, u32[]{:S(2)}) collective-permute-start(f32[2,4,64,128]{3,2,1,0:T(8,128)S(1)} %collective-permute-done.15.refs_2_), channel_id=1, source_target_pairs={{0,4},{4,0},{8,12},{12,8},{16,20},{20,16},{24,28},{28,24},{1,5},{5... | collective-permute-start | bytes 786440 | tf_op jit(solution)/shard_map/ppermute | solution.py:481
  98.4 2.1 %collective-permute-start.19 = (f32[4,16,2048]{2,1,0:T(8,128)S(1)}, f32[4,16,2048]{2,1,0:T(8,128)S(1)}, u32[]{:S(2)}, u32[]{:S(2)}) collective-permute-start(f32[4,16,2048]{2,1,0:T(8,128)S(1)} %get-tuple-element.52), channel_id=1, source_target_pairs={{0,4},{4,0},{8,12},{12,8},{16,20},{20,16},{24,28},{28,24},{1,5},{5... | collective-permute-start | bytes 1572872 | tf_op jit(solution)/shard_map/ppermute | solution.py:481
  100.5 8.3 %collective-permute-start.20 = (f32[16,2048]{1,0:T(8,128)S(1)}, f32[16,2048]{1,0:T(8,128)S(1)}, u32[]{:S(2)}, u32[]{:S(2)}) collective-permute-start(f32[16,2048]{1,0:T(8,128)S(1)} %get-tuple-element.54), channel_id=1, source_target_pairs={{0,8},{4,12},{8,0},{12,4},{16,24},{20,28},{24,16},{28,20},{1,9},{5... | collective-permute-start | bytes 393224 | tf_op jit(solution)/shard_map/ppermute | solution.py:484
  101.7 13.1 %collective-permute-start.21 = (f32[16,2048]{1,0:T(8,128)S(1)}, f32[16,2048]{1,0:T(8,128)S(1)}, u32[]{:S(2)}, u32[]{:S(2)}) collective-permute-start(f32[16,2048]{1,0:T(8,128)S(1)} %get-tuple-element.55), channel_id=1, source_target_pairs={{0,16},{4,20},{8,24},{12,28},{16,0},{20,4},{24,8},{28,12},{1,17},{... | collective-permute-start | bytes 393224 | tf_op jit(solution)/shard_map/ppermute | solution.py:484
  104.8 10.0 %collective-permute-start.22 = (f32[16,2048]{1,0:T(8,128)S(1)}, f32[16,2048]{1,0:T(8,128)S(1)}, u32[]{:S(2)}, u32[]{:S(2)}) collective-permute-start(f32[16,2048]{1,0:T(8,128)S(1)} %get-tuple-element.56), channel_id=1, source_target_pairs={{0,24},{4,28},{8,16},{12,20},{16,8},{20,12},{24,0},{28,4},{1,25},{... | collective-permute-start | bytes 393224 | tf_op jit(solution)/shard_map/ppermute | solution.py:484
  114.8 12.2 %collective-permute-start.25 = (f32[16,2048]{1,0:T(8,128)S(1)}, f32[16,2048]{1,0:T(8,128)S(1)}, u32[]{:S(2)}, u32[]{:S(2)}) collective-permute-start(f32[16,2048]{1,0:T(8,128)S(1)} %add_add_fusion.after_ref.refs_0_), channel_id=1, source_target_pairs={{0,24},{4,28},{8,16},{12,20},{16,8},{20,12},{24,0},{28,4},{1,25},{... | collective-permute-start | bytes 393224 | tf_op jit(solution)/shard_map/ppermute | solution.py:484
  117.3 12.1 %collective-permute-start.24 = (f32[16,2048]{1,0:T(8,128)S(1)}, f32[16,2048]{1,0:T(8,128)S(1)}, u32[]{:S(2)}, u32[]{:S(2)}) collective-permute-start(f32[16,2048]{1,0:T(8,128)S(1)} %add_add_fusion.after_ref.refs_0_), channel_id=1, source_target_pairs={{0,16},{4,20},{8,24},{12,28},{16,0},{20,4},{24,8},{28,12},{1,17},{... | collective-permute-start | bytes 393224 | tf_op jit(solution)/shard_map/ppermute | solution.py:484
  119.1 10.3 %collective-permute-start.23 = (f32[16,2048]{1,0:T(8,128)S(1)}, f32[16,2048]{1,0:T(8,128)S(1)}, u32[]{:S(2)}, u32[]{:S(2)}) collective-permute-start(f32[16,2048]{1,0:T(8,128)S(1)} %add_add_fusion.after_ref.refs_0_), channel_id=1, source_target_pairs={{0,8},{4,12},{8,0},{12,4},{16,24},{20,28},{24,16},{28,20},{1,9},{5... | collective-permute-start | bytes 393224 | tf_op jit(solution)/shard_map/ppermute | solution.py:484
  119.2 24.7 %slice-start = ((s8[8388608]{0:T(1024)(128)(4,1)}), s8[4194304]{0:T(1024)(128)(4,1)S(1)}, s32[]{:S(2)}) async-start(s8[8388608]{0:T(1024)(128)(4,1)} %bitcast.12), calls=%async_computation | async-start | bytes 8388608
  119.3 24.7 %slice-start.2 = ((s8[8388608]{0:T(1024)(128)(4,1)}), s8[4194304]{0:T(1024)(128)(4,1)S(1)}, s32[]{:S(2)}) async-start(s8[8388608]{0:T(1024)(128)(4,1)} %bitcast.14), calls=%async_computation.2 | async-start | bytes 8388608
  126.9 17.0 %collective-permute-start.26 = (f32[16,2048]{1,0:T(8,128)S(1)}, f32[16,2048]{1,0:T(8,128)S(1)}, u32[]{:S(2)}, u32[]{:S(2)}) collective-permute-start(f32[16,2048]{1,0:T(8,128)S(1)} %add_add_fusion.after_ref.refs_0_), channel_id=1, source_target_pairs={{0,4},{4,0},{8,12},{12,8},{16,20},{20,16},{24,28},{28,24},{1,5},{5... | collective-permute-start | bytes 393224 | tf_op jit(solution)/shard_map/ppermute | solution.py:481
  127.0 17.0 %collective-permute-start.29 = (f32[16,2048]{1,0:T(8,128)S(1)}, f32[16,2048]{1,0:T(8,128)S(1)}, u32[]{:S(2)}, u32[]{:S(2)}) collective-permute-start(f32[16,2048]{1,0:T(8,128)S(1)} %collective-permute-done.25.refs_3_), channel_id=1, source_target_pairs={{0,4},{4,0},{8,12},{12,8},{16,20},{20,16},{24,28},{28,24},{1,5},{5... | collective-permute-start | bytes 393224 | tf_op jit(solution)/shard_map/ppermute | solution.py:481
  129.4 14.5 %collective-permute-start.28 = (f32[16,2048]{1,0:T(8,128)S(1)}, f32[16,2048]{1,0:T(8,128)S(1)}, u32[]{:S(2)}, u32[]{:S(2)}) collective-permute-start(f32[16,2048]{1,0:T(8,128)S(1)} %collective-permute-done.24.refs_2_), channel_id=1, source_target_pairs={{0,4},{4,0},{8,12},{12,8},{16,20},{20,16},{24,28},{28,24},{1,5},{5... | collective-permute-start | bytes 393224 | tf_op jit(solution)/shard_map/ppermute | solution.py:481
  129.5 14.5 %collective-permute-start.27 = (f32[16,2048]{1,0:T(8,128)S(1)}, f32[16,2048]{1,0:T(8,128)S(1)}, u32[]{:S(2)}, u32[]{:S(2)}) collective-permute-start(f32[16,2048]{1,0:T(8,128)S(1)} %collective-permute-done.23.refs_1_), channel_id=1, source_target_pairs={{0,4},{4,0},{8,12},{12,8},{16,20},{20,16},{24,28},{28,24},{1,5},{5... | collective-permute-start | bytes 393224 | tf_op jit(solution)/shard_map/ppermute | solution.py:481
  130.0 14.0 %slice-start.1 = ((s8[8388608]{0:T(1024)(128)(4,1)}), s8[4194304]{0:T(1024)(128)(4,1)S(1)}, s32[]{:S(2)}) async-start(s8[8388608]{0:T(1024)(128)(4,1)} %bitcast.12), calls=%async_computation.1 | async-start | bytes 8388608
  130.0 14.0 %slice-start.3 = ((s8[8388608]{0:T(1024)(128)(4,1)}), s8[4194304]{0:T(1024)(128)(4,1)S(1)}, s32[]{:S(2)}) async-start(s8[8388608]{0:T(1024)(128)(4,1)} %bitcast.14), calls=%async_computation.3 | async-start | bytes 8388608

commit v3 on v2

--- a/solution.py
+++ b/solution.py
@@ -12,6 +12,7 @@
 HIGHEST = lax.Precision.HIGHEST
 RANK = 128
 VMEM_LIMIT = 50 * 1024 * 1024
+LEFT_LIMIT = 14 * 1024 * 1024
 SMALL_LIMIT = 6 * 1024 * 1024
 MERGED_LIMIT = 8 * 1024 * 1024
 RIGHT_LIMIT = 11 * 1024 * 1024
@@ -51,8 +52,7 @@
     args = [*after, *args]
     return pl.pallas_call(
         functools.partial(skipping, len(after), body),
-        in_specs=[pl.BlockSpec(memory_space=pl.ANY)] * len(after)
-        + [pl.BlockSpec(memory_space=pltpu.VMEM)] * (len(args) - len(after)),
+        in_specs=[pl.BlockSpec(memory_space=pltpu.VMEM)] * len(args),
         out_specs=[pl.BlockSpec(memory_space=pltpu.VMEM)] * len(outs),
         out_shape=[jax.ShapeDtypeStruct(*out) for out in outs],
         compiler_params=params(limit),
@@ -61,74 +61,107 @@
     )(*args)
 
 
-def u_kernel(g_ref, q_ref, ucat_ref, qcat_ref):
-    @pl.when(pl.program_id(0) == 0)
-    def _():
-        qcat_ref[...] = split_rows(q_ref[...].T)
-
-    ucat_ref[...] = split_rows(fold(dot(qcat_ref[...], g_ref[...], ROWS_BY_ROWS)))
-
-
-def grads_by_q(g, q):
-    tok, cols = g.shape
-    tile = tok // 2
-    return pl.pallas_call(
-        u_kernel,
-        grid=(tok // tile,),
-        in_specs=[
-            pl.BlockSpec((tile, cols), lambda i: (i, 0)),
-            pl.BlockSpec((cols, RANK), lambda i: (0, 0)),
-        ],
-        out_specs=[
-            pl.BlockSpec((2 * RANK, tile), lambda i: (0, i)),
-            pl.BlockSpec((2 * RANK, cols), lambda i: (0, 0)),
-        ],
-        out_shape=[
-            jax.ShapeDtypeStruct((2 * RANK, tok), BF16),
-            jax.ShapeDtypeStruct((2 * RANK, cols), BF16),
-        ],
-        compiler_params=params(),
-        cost_estimate=cost(4 * tok * cols * RANK, tok * cols * 2 + cols * RANK * 8),
-        name="grads_by_q",
-    )(g, q)
-
-
-def p_kernel(nz, ids_ref, a_ref, e_ref, ucat_ref, qcat_ref, p_ref, acc_ref):
-    acc = dot(qcat_ref[...], e_ref[...], ROWS_BY_ROWS) + dot(ucat_ref[...], a_ref[...])
-    acc_ref[...] = fold(acc).T
-    rows = p_ref.shape[2]
-    for k in range(nz):
-        start = pl.multiple_of((ids_ref[2] ^ k) * rows, rows)
-        p_ref[0, k] = acc_ref[pl.ds(start, rows), :]
-
-
-def left_terms(ids, a, e, ucat, qcat, kc, nm, nz):
+STEPS = 8
+
+
+def copies_of_half(a_hbm, e_hbm, a_ref, e_ref, sems, half):
+    rows = e_ref.shape[0]
+    tile = rows // STEPS
+    copies = []
+    for i in range(STEPS):
+        here = pl.ds(i * tile, tile)
+        there = pl.ds(pl.multiple_of(half * rows + i * tile, tile), tile)
+        copies.append(
+            (
+                pltpu.make_async_copy(e_hbm.at[there, :], e_ref.at[here, :], sems.at[2 * i]),
+                pltpu.make_async_copy(a_hbm.at[:, there], a_ref.at[:, here], sems.at[2 * i + 1]),
+            )
+        )
+    return copies
+
+
+def p_of_half(ids_ref, copies, a_ref, e_ref, ucat_ref, qcat_ref, p_ref):
+    nz, small = p_ref.shape[1:3]
+    tile = e_ref.shape[0] // STEPS
+    for i, (e_copy, a_copy) in enumerate(copies):
+        here = pl.ds(i * tile, tile)
+        e_copy.wait()
+        acc = dot(qcat_ref[...], e_ref[here, :], ROWS_BY_ROWS)
+        a_copy.wait()
+        acc += dot(ucat_ref[...], a_ref[:, here])
+        p_tile = fold(acc).T
+        for k in range(tile // small):
+            block = i * (tile // small) + k
+            p_ref[(block // nz) ^ ids_ref[1], (block % nz) ^ ids_ref[2]] = p_tile[k * small : (k + 1) * small]
+
+
+def far_kernel(
+    ids_ref, q_hbm, g_hbm, a_hbm, e_hbm, p_ref, a_ref, e_ref, g_ref, ucat_ref, qcat_ref, q_ref, sems, first_sems
+):
+    tok = g_ref.shape[0]
+    q_copy = pltpu.make_async_copy(q_hbm, q_ref, first_sems.at[0])
+    q_copy.start()
+    g_copies = []
+    for i in range(2):
+        at = pl.ds(i * (tok // 2), tok // 2)
+        g_copies.append(pltpu.make_async_copy(g_hbm.at[at, :], g_ref.at[at, :], first_sems.at[1 + i]))
+        g_copies[-1].start()
+    copies = copies_of_half(a_hbm, e_hbm, a_ref, e_ref, sems, ids_ref[0] ^ 1)
+    for pair in copies:
+        for copy in pair:
+            copy.start()
+    q_copy.wait()
+    qcat_ref[...] = split_rows(q_ref[...].T)
+    for i in range(2):
+        at = pl.ds(i * (tok // 2), tok // 2)
+        g_copies[i].wait()
+        ucat_ref[:, at] = split_rows(fold(dot(qcat_ref[...], g_ref[at, :], ROWS_BY_ROWS)))
+    p_of_half(ids_ref, copies, a_ref, e_ref, ucat_ref, qcat_ref, p_ref)
+
+
+def near_kernel(ids_ref, ucat_ref, qcat_ref, a_hbm, e_hbm, p_ref, a_ref, e_ref, sems):
+    copies = copies_of_half(a_hbm, e_hbm, a_ref, e_ref, sems, ids_ref[0])
+    for pair in copies:
+        for copy in pair:
+            copy.start()
+    p_of_half(ids_ref, copies, a_ref, e_ref, ucat_ref, qcat_ref, p_ref)
+
+
+def left_terms(ids, q, g, a, e, nm, nz, before=None):
     tok, rows = a.shape
     cols = e.shape[1]
-    tile = rows // (2 * nm)
-
-    def block(j, ids_ref):
-        return (ids_ref[0] ^ kc) * nm + (ids_ref[1] ^ j)
-
+    vmem = pl.BlockSpec(memory_space=pltpu.VMEM)
+    hbm = pl.BlockSpec(memory_space=pltpu.HBM)
+    outs = [
+        pltpu.VMEM((nm, nz, rows // (2 * nm * nz), RANK), F32),
+        pltpu.VMEM((tok, rows // 2), BF16),
+        pltpu.VMEM((rows // 2, cols), BF16),
+    ]
+    scratch = [pltpu.SemaphoreType.DMA((2 * STEPS,))]
+    if before is None:
+        body, specs, args = far_kernel, [hbm] * 4, (q, g, a, e)
+        outs += [
+            pltpu.VMEM((tok, cols), BF16),
+            pltpu.VMEM((2 * RANK, tok), BF16),
+            pltpu.VMEM((2 * RANK, cols), BF16),
+        ]
+        scratch = [pltpu.VMEM((cols, RANK), F32)] + scratch + [pltpu.SemaphoreType.DMA((3,))]
+    else:
+        body, specs, args = near_kernel, [vmem] * 2 + [hbm] * 2, (*before, a, e)
     return pl.pallas_call(
-        functools.partial(p_kernel, nz),
+        body,
         grid_spec=pltpu.PrefetchScalarGridSpec(
             num_scalar_prefetch=1,
-            grid=(nm,),
-            in_specs=[
-                pl.BlockSpec((tok, tile), lambda j, ids_ref: (0, block(j, ids_ref))),
-                pl.BlockSpec((tile, cols), lambda j, ids_ref: (block(j, ids_ref), 0)),
-                pl.BlockSpec((2 * RANK, tok), lambda j, ids_ref: (0, 0)),
-                pl.BlockSpec((2 * RANK, cols), lambda j, ids_ref: (0, 0)),
-            ],
-            out_specs=pl.BlockSpec((1, nz, tile // nz, RANK), lambda j, ids_ref: (j, 0, 0, 0)),
-            scratch_shapes=[pltpu.VMEM((tile, RANK), F32)],
+            grid=(),
+            in_specs=specs,
+            out_specs=[vmem] * len(outs),
+            scratch_shapes=scratch,
         ),
-        out_shape=jax.ShapeDtypeStruct((nm, nz, tile // nz, RANK), F32),
-        compiler_params=params(),
+        out_shape=outs,
+        compiler_params=params(LEFT_LIMIT),
         cost_estimate=cost(2 * rows * RANK * (tok + cols), rows * (tok + cols)),
         name="left_terms",
-    )(ids, a, e, ucat, qcat)
+    )(ids, *args)
 
 
 def first_sum_kernel(keeps, sends, near_ref, far_ref, *outs):
@@ -228,80 +261,85 @@
         members = [members[h] + came_members[h] for h in range(2)]
 
 
-def merged_kernel(part, after_ref, a_ref, e_ref, g_ref, out_ref):
-    tok, cols = g_ref.shape
-    rows = out_ref.shape[0]
-    tile = rows // 4
-
-    def body(a_tile, e_tile):
-        start = pl.multiple_of(pl.program_id(0) * tile, tile)
-        out_ref[pl.ds(start, tile), :] = dot(a_tile[...], g_ref[...], ((0,), (0,))) + e_tile[...].astype(F32)
-
-    pltpu.emit_pipeline(
-        body,
-        grid=(4,),
-        in_specs=[
-            pl.BlockSpec((tok, tile), lambda i: (0, part * 4 + i)),
-            pl.BlockSpec((tile, cols), lambda i: (part * 4 + i, 0)),
-        ],
-    )(a_ref, e_ref)
-
-
-def merged_part(a, e, g, part, parts, after):
-    tok, rows = a.shape
+def merged_kernel(part, in_hbm, after_ref, a_ref, e_ref, g_ref, out_ref, done_ref, a_t):
+    done_ref[...] = jnp.zeros_like(done_ref)
+    rows, cols = out_ref.shape
+    chunk = min(cols, 512)
+    at = pl.ds(part * rows, rows)
+    a_t[...] = a_ref[:, at].T
+
+    def values(i):
+        here = pl.ds(pl.multiple_of(i * chunk, chunk), chunk)
+        return here, dot(a_t[...], g_ref[:, here]) + e_ref[at, here].astype(F32)
+
+    if in_hbm:
+
+        def body(out_tile):
+            out_tile[...] = values(pl.program_id(0))[1]
+
+        pltpu.emit_pipeline(
+            body, grid=(cols // chunk,), in_specs=[], out_specs=[pl.BlockSpec((rows, chunk), lambda i: (0, i))]
+        )(out_ref)
+    else:
+
+        @pl.loop(0, cols // chunk)
+        def _(i):
+            here, value = values(i)
+            out_ref[:, here] = value
+
+
+def merged_part(a, e, g, part, in_hbm, after):
+    tok, half = a.shape
     cols = e.shape[1]
+    rows = half // 2
+    place = pltpu.HBM if in_hbm else pltpu.VMEM
     return pl.pallas_call(
-        functools.partial(merged_kernel, part),
-        in_specs=[pl.BlockSpec(memory_space=pl.ANY)]
-        + [pl.BlockSpec(memory_space=pltpu.HBM)] * 2
-        + [pl.BlockSpec(memory_space=pltpu.VMEM)],
-        out_specs=pl.BlockSpec(memory_space=pltpu.VMEM),
-        out_shape=pltpu.VMEM((rows // parts, cols), F32),
+        functools.partial(merged_kernel, part, in_hbm),
+        in_specs=[pl.BlockSpec(memory_space=pl.ANY)] + [pl.BlockSpec(memory_space=pltpu.VMEM)] * 3,
+        out_specs=[pl.BlockSpec(memory_space=place), pl.BlockSpec(memory_space=pltpu.VMEM)],
+        out_shape=[place((rows, cols), F32), jax.ShapeDtypeStruct((8, RANK), F32)],
+        scratch_shapes=[pltpu.VMEM((rows, tok), BF16)],
         compiler_params=params(MERGED_LIMIT),
-        cost_estimate=cost(2 * tok * cols * rows // parts, (rows * cols * 2 + rows * tok * 2) // parts),
+        cost_estimate=cost(2 * tok * cols * rows, rows * cols * 2),
         name="merged",
     )(after, a, e, g)
 
 
-def q_kernel(owners, kc, nm, nz, last, ids_ref, *refs):
+def q_kernel(owners, nm, nz, last, ids_ref, after_ref, *refs):
     pieces, refs = refs[:4], refs[4:]
     if last:
-        v_in, q_in, gram_in, a_ref, e_ref, g_ref, send_ref, keep_ref, gram_ref, p_half, v_acc, q_acc, gram_acc = refs
-        v_acc[...], q_acc[...], gram_acc[...] = v_in[...], q_in[...], gram_in[...]
+        v_in, q_in, gram_in, a_ref, e_ref, g_ref, send_ref, keep_ref, gram_ref, p_half, pcat, q_acc = refs
     else:
-        a_ref, e_ref, v_acc, q_acc, gram_acc, p_half = refs
-        for acc in (v_acc, q_acc, gram_acc):
-            acc[...] = jnp.zeros_like(acc)
+        a_ref, e_ref, v_ref, q_acc, gram_ref, p_half, pcat = refs
     rows = pieces[0].shape[2]
-    tok, cols = a_ref.shape[0], e_ref.shape[1]
-    tile = p_half.shape[0] // nm
+    cols = e_ref.shape[1]
+    chunk = min(cols, 512)
     for piece, (half, members) in zip(pieces, owners):
         for i, km in enumerate(members):
             for k in range(nz):
                 start = ((ids_ref[1] ^ km) * nz + (ids_ref[2] ^ k)) * (2 * rows) + half * rows
                 p_half[pl.ds(pl.multiple_of(start, rows), rows), :] = piece[i, k]
-    first = (ids_ref[0] ^ kc) * nm
-
-    def body(a_tile, e_tile):
-        start = pl.multiple_of(pl.program_id(0) * tile, tile)
-        pcat = split_rows(p_half[pl.ds(start, tile), :].T)
-        v_acc[...] += fold(dot(pcat, a_tile[...], ROWS_BY_ROWS))
-        q_acc[...] += fold(dot(pcat, e_tile[...]))
-        gram_acc[...] += dot(pcat, pcat, ROWS_BY_ROWS)
-
-    pltpu.emit_pipeline(
-        body,
-        grid=(nm,),
-        in_specs=[
-            pl.BlockSpec((tok, tile), lambda j: (0, first + j)),
-            pl.BlockSpec((tile, cols), lambda j: (first + j, 0)),
-        ],
-    )(a_ref, e_ref)
-
+    pcat[...] = split_rows(p_half[...].T)
+    v = fold(dot(pcat[...], a_ref[...], ROWS_BY_ROWS))
+    gram = dot(pcat[...], pcat[...], ROWS_BY_ROWS)
     if last:
-        q_acc[...] += fold(dot(split_rows(v_acc[...]), g_ref[...]))
-        whole = fold(gram_acc[...])
+        vcat = split_rows(v + v_in[...])
+        whole = fold(gram + gram_in[...])
         gram_ref[...] = whole[:, :RANK] + whole[:, RANK:]
+    else:
+        v_ref[...] = v
+        gram_ref[...] = gram
+
+    for i in range(cols // chunk):
+        here = pl.ds(i * chunk, chunk)
+        q = dot(pcat[...], e_ref[:, here])
+        if last:
+            q += dot(vcat, g_ref[:, here])
+            q_acc[:, here] = fold(q) + q_in[:, here]
+        else:
+            q_acc[:, here] = fold(q)
+
+    if last:
         small = send_ref.shape[1]
         for out, flip in ((send_ref, 1), (keep_ref, 0)):
             for k in range(nz):
@@ -309,38 +347,35 @@
                 out[k] = q_acc[pl.ds(pl.multiple_of(start, small), small), :]
 
 
-def right_terms(ids, pieces, owners, a, e, g, kc, nm, before=None):
-    tok, rows = a.shape
+def right_terms(ids, pieces, owners, a, e, g, nm, after, before=None):
+    tok, half = a.shape
     cols = e.shape[1]
     nz = pieces[0].shape[1]
     last = before is not None
     vmem = pl.BlockSpec(memory_space=pltpu.VMEM)
-    hbm = pl.BlockSpec(memory_space=pltpu.HBM)
     sums = [(RANK, tok), (RANK, cols), (2 * RANK, 2 * RANK)]
-    scratch = [pltpu.VMEM((rows // 2, RANK), F32)]
+    scratch = [pltpu.VMEM((half, RANK), F32), pltpu.VMEM((2 * RANK, half), BF16)]
     if last:
-        specs = [vmem] * 7 + [hbm] * 2 + [vmem]
         args = [*pieces, *before, a, e, g]
         outs = [(nz, RANK // (2 * nz), cols)] * 2 + [(RANK, RANK)]
-        scratch += [pltpu.VMEM(shape, F32) for shape in sums]
+        scratch += [pltpu.VMEM((RANK, cols), F32)]
     else:
-        specs = [vmem] * 4 + [hbm] * 2
         args = [*pieces, a, e]
         outs = sums
     return pl.pallas_call(
-        functools.partial(q_kernel, owners, kc, nm, nz, last),
+        functools.partial(q_kernel, owners, nm, nz, last),
         grid_spec=pltpu.PrefetchScalarGridSpec(
             num_scalar_prefetch=1,
             grid=(),
-            in_specs=specs,
+            in_specs=[pl.BlockSpec(memory_space=pl.ANY)] + [vmem] * len(args),
             out_specs=[vmem] * 3,
             scratch_shapes=scratch,
         ),
         out_shape=[jax.ShapeDtypeStruct(shape, F32) for shape in outs],
         compiler_params=params(RIGHT_LIMIT),
-        cost_estimate=cost(2 * rows * RANK * (tok + cols), rows * (tok + cols)),
+        cost_estimate=cost(4 * half * RANK * (tok + cols), half * (tok + cols)),
         name="right_terms",
-    )(ids, *args)
+    )(ids, after, *args)
 
 
 def chol_inverse_kernel(gram_ref, out_ref):
@@ -368,7 +403,7 @@
         for piece, (half, members) in zip(pieces[4 * h : 4 * h + 4], owners):
             for i, km in enumerate(members):
                 for k in range(nz):
-                    block = ((ids_ref[0] ^ h) * nm + (ids_ref[1] ^ km)) * nz + (ids_ref[2] ^ k)
+                    block = (h * nm + (ids_ref[1] ^ km)) * nz + (ids_ref[2] ^ k)
                     start = block * (2 * rows) + half * rows
                     p_all[pl.ds(pl.multiple_of(start, rows), rows), :] = piece[i, k]
     inv_hi = inv_ref[...].T.astype(BF16)
@@ -405,9 +440,10 @@
     )(ids, after, *pieces, inv)
 
 
-def final_kernel(nz, scale, tile, ids_ref, *refs):
+def final_kernel(nz, scale, ids_ref, *refs):
     pieces, refs = refs[: 2 * nz], refs[2 * nz :]
-    inv_ref, phat_ref, parts, (err_ref, qnew_ref, q_sum, q_cat) = refs[0], refs[1], refs[2:6], refs[6:]
+    inv_ref, phat_ref, parts = refs[0], refs[1], refs[2:6]
+    err_ref, qnew_hbm, q_sum, q_cat, qnew_ref, sem = refs[6:]
     small = pieces[0].shape[0]
     for h in range(2):
         for k in range(nz):
@@ -416,26 +452,33 @@
     q_t = scale * lax.dot_general(
         inv_ref[...], q_sum[...], (((1,), (0,)), ((), ())), precision=HIGHEST, preferred_element_type=F32
     )
-    qnew_ref[...] = q_t.T
     hi = q_t.astype(BF16)
     lo = (q_t - hi.astype(F32)).astype(BF16)
     q_cat[...] = jnp.concatenate([hi, hi, lo, lo], axis=0)
+    qnew_ref[...] = q_t.T
+    copy = pltpu.make_async_copy(qnew_ref, qnew_hbm, sem)
+    copy.start()
     part_rows, cols = parts[0].shape
-    steps = part_rows // tile
-    for number, merged in enumerate(parts):
-
-        def body(out_tile):
-            start = pl.multiple_of(pl.program_id(0) * tile, tile)
-            x = phat_ref[pl.ds(pl.multiple_of(number * part_rows + start, tile), tile), :]
-            approx = dot(jnp.concatenate([x, x], axis=1), q_cat[...])
-            out_tile[0] = (merged[pl.ds(start, tile), :] - approx).astype(BF16)
-
-        pltpu.emit_pipeline(
-            body,
-            grid=(steps,),
-            in_specs=[],
-            out_specs=[pl.BlockSpec((1, tile, cols), lambda i, number=number: (0, number * steps + i, 0))],
-        )(err_ref)
+    chunk = min(cols, 512)
+    own = ids_ref[0]
+
+    def body(out_tile):
+        here = pl.ds(pl.multiple_of(pl.program_id(1) * chunk, chunk), chunk)
+        for number, merged in enumerate(parts):
+
+            @pl.when(pl.program_id(0) == number)
+            def _():
+                x = phat_ref[pl.ds(number * part_rows, part_rows), :]
+                approx = dot(jnp.concatenate([x, x], axis=1), q_cat[:, here])
+                out_tile[0] = (merged[:, here] - approx).astype(BF16)
+
+    pltpu.emit_pipeline(
+        body,
+        grid=(len(parts), cols // chunk),
+        in_specs=[],
+        out_specs=[pl.BlockSpec((1, part_rows, chunk), lambda i, j: (0, i ^ (own * 2), j))],
+    )(err_ref)
+    copy.wait()
 
 
 def finish(ids, pieces, inv, phat, parts, replicas):
@@ -445,13 +488,18 @@
     vmem = pl.BlockSpec(memory_space=pltpu.VMEM)
     hbm = pl.BlockSpec(memory_space=pltpu.HBM)
     return pl.pallas_call(
-        functools.partial(final_kernel, nz, 1.0 / replicas, rows // 16),
+        functools.partial(final_kernel, nz, 1.0 / replicas),
         grid_spec=pltpu.PrefetchScalarGridSpec(
             num_scalar_prefetch=1,
             grid=(),
-            in_specs=[vmem] * (2 * nz + 1) + [vmem] + [vmem] * len(parts),
-            out_specs=[hbm, vmem],
-            scratch_shapes=[pltpu.VMEM((RANK, cols), F32), pltpu.VMEM((4 * RANK, cols), BF16)],
+            in_specs=[vmem] * (2 * nz + 2 + len(parts)),
+            out_specs=[hbm, hbm],
+            scratch_shapes=[
+                pltpu.VMEM((RANK, cols), F32),
+                pltpu.VMEM((4 * RANK, cols), BF16),
+                pltpu.VMEM((cols, RANK), F32),
+                pltpu.SemaphoreType.DMA,
+            ],
         ),
         out_shape=[jax.ShapeDtypeStruct((1, rows, cols), BF16), jax.ShapeDtypeStruct((cols, RANK), F32)],
         compiler_params=params(FINAL_LIMIT),
@@ -467,9 +515,9 @@
 
 
 def per_device(n_dp, n_mp, activations, out_grads, error_fb, q_prev):
-    a, g, e = activations[0], out_grads[0], error_fb[0]
-    a_hbm = pltpu.with_memory_space_constraint(a, pltpu.HBM)
-    e_hbm = pltpu.with_memory_space_constraint(e, pltpu.HBM)
+    a, g, e, q = [
+        pltpu.with_memory_space_constraint(x, pltpu.HBM) for x in (activations[0], out_grads[0], error_fb[0], q_prev)
+    ]
     rows = a.shape[1]
     nz = n_dp // 2
     dp, mp = lax.axis_index("dp"), lax.axis_index("mp")
@@ -486,15 +534,17 @@
     def to_mp(x, k):
         return lax.ppermute(x, "mp", [(i, i ^ k) for i in range(n_mp)])
 
-    ucat, qcat = grads_by_q(g, q_prev)
-    p_far = left_terms(ids, a, e, ucat, qcat, 1, n_mp, nz)
+    p_far, a_far, e_far, g_here, ucat, qcat = left_terms(ids, q, g, a, e, n_mp, nz)
     p_arrived = to_core(p_far)
-    p_near = left_terms(ids, a, e, ucat, qcat, 0, n_mp, nz)
+    p_near, a_near, e_near = left_terms(ids, q, g, a, e, n_mp, nz, (ucat, qcat))
     parts = []
 
     def beside(sent):
-        parts.append(merged_part(a_hbm, e_hbm, g, len(parts), 4, sent))
-        return parts[-1]
+        number = len(parts)
+        mine = (a_near, e_near) if number < 2 else (a_far, e_far)
+        part, done = merged_part(*mine, g_here, number % 2, True, sent)
+        parts.append(part)
+        return done
 
     by_z = scatter_over_mp(p_near, p_arrived, to_mp, orders, beside)
     done = [beside(by_z[0])]
@@ -503,20 +553,23 @@
     done = [beside(p_own)]
     p_pieces = [p_own] + [to_z(p_own, k) for k in range(1, nz)]
     near, owners = gather_over_mp(p_pieces, to_mp, orders, done)
-    beside(near[0])
+    done = beside(near[0])
     far = [to_core(x) for x in near]
 
-    half = right_terms(ids, near, owners, a_hbm, e_hbm, g, 0, n_mp)
-    q_send, q_keep, gram = right_terms(ids, far, owners, a_hbm, e_hbm, g, 1, n_mp, half)
+    half = right_terms(ids, near, owners, a_near, e_near, g_here, n_mp, done)
+    q_send, q_keep, gram = right_terms(ids, far, owners, a_far, e_far, g_here, n_mp, done, half)
 
     piece = (q_keep.shape[1:], F32)
     q_by_z = in_vmem(functools.partial(q_sum_kernel, nz), [piece] * nz, [q_keep, to_core(q_send)], "q_sum")
-    q_own = q_by_z[0] + sum(to_z(q_by_z[k], k) for k in range(1, nz))
+    square = ((RANK, RANK), F32)
+    [inv] = in_vmem(
+        chol_inverse_kernel, [square], [gram], "chol_inverse", after=[q_by_z[0]], work=cost(2 * 10**10, 10**5)
+    )
+    came = [to_z(q_by_z[k], k) for k in range(1, nz)]
+    [q_own] = in_vmem(own_sum_kernel, [piece], [q_by_z[0], *came], "q_own", after=[inv])
     q_near = [q_own] + [to_z(q_own, k) for k in range(1, nz)]
     q_pieces = q_near + [to_core(x) for x in q_near]
 
-    square = ((RANK, RANK), F32)
-    [inv] = in_vmem(chol_inverse_kernel, [square], [gram], "chol_inverse", work=cost(2 * 10**10, 10**5))
     phat = left_factor(ids, near + far, owners, inv, rows, n_mp, nz, q_own)
     new_error, q_new = finish(ids, q_pieces, inv, phat, parts, n_dp)
     return new_error, q_new

time: 164 us -> 150 us (0.915)
  waiting for transfers between devices: 28.8 us -> 21.8 us
  local copies, waits for them, and re-layouts: 4.63 us -> 0.04 us
    ppermute x8, waiting for transfers between devices: 15.5 us -> 10.3 us  [to_mp(): return lax.ppermute(x, 'mp', [(i, i ^ k) for i in range(n_mp)])]
    unnamed x16, local copies, waits for them, and re-layouts: 4.63 us -> 0.04 us
    ppermute x12, waiting for transfers between devices: 11.7 us -> 9.88 us  [to_z(): return lax.ppermute(x, 'dp', [(i, i ^ 2 * k) for i in range(n_dp)])]
    pallas_call x10 -> x9, Pallas kernels: 84.5 us -> 83.2 us  [the longest x4 28.9 us: merged_part(): pl.pallas_call(functools.partial(merged_kernel, part, in_hbm), in_specs=[...]
    pallas_call x8 -> x9, Pallas kernels: 11.1 us -> 11.1 us  [in_vmem(): pl.pallas_call(functools.partial(skipping, len(after), body), in_specs=[p...]
  transfers between devices with their start and end apart: 30 -> 30, of which waited for: 10 -> 7; matrix products, arithmetic and copies ran while one was open for 0% -> 0% of each run, Pallas kernels for 36% -> 39%
where the time goes in v3:
time: 150 us
  Pallas kernels  97.7 us (65%)
  starting transfers between devices  29 us (19%)
  waiting for transfers between devices  21.8 us (15%)
    pallas_call x4, Pallas kernels, merged_part(): pl.pallas_call(functools.partial(merged_kernel, part, in_hbm), in_specs=[...  28.9 us
    pallas_call x2, Pallas kernels, left_terms(): pl.pallas_call(body, grid_spec=pltpu.PrefetchScalarGridSpec(num_scalar_pr...  28.2 us
    ppermute x12, starting transfers between devices, to_z(): return lax.ppermute(x, 'dp', [(i, i ^ 2 * k) for i in range(n_dp)])  17.8 us
    pallas_call x1, Pallas kernels, finish(): pl.pallas_call(functools.partial(final_kernel, nz, 1.0 / replicas), grid_...  16 us
    pallas_call x9, Pallas kernels, in_vmem(): pl.pallas_call(functools.partial(skipping, len(after), body), in_specs=[p...  11.1 us
    ppermute x8, waiting for transfers between devices, to_mp(): return lax.ppermute(x, 'mp', [(i, i ^ k) for i in range(n_mp)])  10.3 us
    pallas_call x2, Pallas kernels, right_terms(): pl.pallas_call(functools.partial(q_kernel, owners, nm, nz, last), grid_sp...  10 us
    ppermute x12, waiting for transfers between devices, to_z(): return lax.ppermute(x, 'dp', [(i, i ^ 2 * k) for i in range(n_dp)])  9.88 us
  transfers between devices with their start and end apart: 30, of which 7 were waited for; matrix products, arithmetic and copies ran while one was open for 0% of the time, Pallas kernels for 39%

profile of v3, /device:TPU:0, one launch (start us, length us, event | category | flops | bytes accessed | tf_op | source)
XLA Modules:
  0.0 149.8 jit_solution(5888423751299158994)
XLA Ops:
  0.6 0.1 pad_add_fusion.ids_ref
  0.7 16.9 %left_terms.2 = (f32[4,4,128,128]{3,2,1,0:T(8,128)S(1)}, bf16[1024,2048]{1,0:T(8,128)(2,1)S(1)}, bf16[2048,2048]{1,0:T(8,128)(2,1)S(1)}, bf16[1024,2048]{1,0:T(8...) custom-call(s32[3]{0:T(128)S(1)} %pad_add_fusion.ids_ref, f32[2048,128]{1,0:T(8,128)} %q_hbm.1, ...), custom_call_target="tpu_custom_call" | custom-call | flops 3221225472 | bytes 12582912 | tf_op jit(solution)/shard_map/left_terms/pallas_call | solution.py:151
  17.6 0.5 collective-permute-start
  18.2 11.3 %left_terms.3 = (f32[4,4,128,128]{3,2,1,0:T(8,128)S(1)}, bf16[1024,2048]{1,0:T(8,128)(2,1)S(1)}, bf16[2048,2048]{1,0:T(8,128)(2,1)S(1)}) custom-call(s32[3]{0:T(128)S(1)} %pad_add_fusion.ids_ref, bf16[256,1024]{1,0:T(8,128)(2,1)S(1)} %get-tuple-element.45.ucat_ref, bf16[256,2048]{1,0:T(8,128)(2,1)S(1)} %get-tuple-element.46.qcat_ref, ...), custom_call_target="tpu_custom_call" | custom-call | flops 3221225472 | bytes 12582912 | tf_op jit(solution)/shard_map/left_terms/pallas_call | solution.py:151
  29.5 0.1 first_sum.1
  29.6 2.6 %collective-permute-start.1 = (f32[2,4,64,128]{3,2,1,0:T(8,128)S(1)}, f32[2,4,64,128]{3,2,1,0:T(8,128)S(1)}, u32[]{:S(2)}, u32[]{:S(2)}) collective-permute-start(f32[2,4,64,128]{3,2,1,0:T(8,128)S(1)} %get-tuple-element.54), channel_id=1, source_target_pairs={{0,1},{1,0},{2,3},{3,2},{4,5},{5,4},{6,7},{7,6},{8,9},{9,8},{10,11... | collective-permute-start | bytes 786440 | tf_op jit(solution)/shard_map/ppermute | solution.py:535
  32.1 1.5 %collective-permute-start.2 = (f32[2,4,64,128]{3,2,1,0:T(8,128)S(1)}, f32[2,4,64,128]{3,2,1,0:T(8,128)S(1)}, u32[]{:S(2)}, u32[]{:S(2)}) collective-permute-start(f32[2,4,64,128]{3,2,1,0:T(8,128)S(1)} %get-tuple-element.56), channel_id=1, source_target_pairs={{0,2},{1,3},{2,0},{3,1},{4,6},{5,7},{6,4},{7,5},{8,10},{9,11},{10,... | collective-permute-start | bytes 786440 | tf_op jit(solution)/shard_map/ppermute | solution.py:535
  33.7 7.2 %merged.4 = (f32[1024,2048]{1,0:T(8,128)}, f32[8,128]{1,0:T(8,128)S(1)}) custom-call(f32[2,4,64,128]{3,2,1,0:T(8,128)S(1)} %get-tuple-element.49.after_ref.refs_1_, bf16[1024,2048]{1,0:T(8,128)(2,1)S(1)} %get-tuple-element.50.a_ref.refs_4_, bf16[2048,2048]{1,0:T(8,128)(2,1)S(1)} %get-tuple-element.51.e_ref.refs_5_, ...), custom_call_target="tpu_custom_call" | custom-call | flops 4294967296 | bytes 4194304 | tf_op jit(solution)/shard_map/merged/pallas_call | solution.py:296
  40.9 0.1 next_sum.1
  41.0 1.2 collective-permute-start.3
  42.2 0.5 collective-permute-start.4
  42.7 3.6 %collective-permute-done.3.refs_1_ = f32[1,4,64,128]{3,2,1,0:T(8,128)S(1)} collective-permute-done((f32[1,4,64,128]{3,2,1,0:T(8,128)S(1)}, f32[1,4,64,128]{3,2,1,0:T(8,128)S(1)}, u32[]{:S(2)}, u32[]{:S(2)}) %collective-permute-start.3) | collective-permute-done | bytes 131104 | tf_op jit(solution)/shard_map/ppermute | solution.py:535
  46.4 0.8 collective-permute-done.4.refs_3_
  47.2 1.6 %collective-permute-start.5 = (f32[128,128]{1,0:T(8,128)S(1)}, f32[128,128]{1,0:T(8,128)S(1)}, u32[]{:S(2)}, u32[]{:S(2)}) collective-permute-start(f32[128,128]{1,0:T(8,128)S(1)} %get-tuple-element.63), channel_id=1, source_target_pairs={{0,8},{4,12},{8,0},{12,4},{16,24},{20,28},{24,16},{28,20},{1,9},{5... | collective-permute-start | bytes 196616 | tf_op jit(solution)/shard_map/ppermute | solution.py:532
  48.9 2.6 %collective-permute-start.6 = (f32[128,128]{1,0:T(8,128)S(1)}, f32[128,128]{1,0:T(8,128)S(1)}, u32[]{:S(2)}, u32[]{:S(2)}) collective-permute-start(f32[128,128]{1,0:T(8,128)S(1)} %get-tuple-element.64), channel_id=1, source_target_pairs={{0,16},{4,20},{8,24},{12,28},{16,0},{20,4},{24,8},{28,12},{1,17},{... | collective-permute-start | bytes 196616 | tf_op jit(solution)/shard_map/ppermute | solution.py:532
  51.4 0.2 collective-permute-start.7
  51.7 7.3 %merged.5 = (f32[1024,2048]{1,0:T(8,128)}, f32[8,128]{1,0:T(8,128)S(1)}) custom-call(f32[128,128]{1,0:T(8,128)S(1)} %get-tuple-element.61.after_ref.refs_1_, bf16[1024,2048]{1,0:T(8,128)(2,1)S(1)} %get-tuple-element.50.a_ref.refs_4_, bf16[2048,2048]{1,0:T(8,128)(2,1)S(1)} %get-tuple-element.51.e_ref.refs_5_, ...), custom_call_target="tpu_custom_call" | custom-call | flops 4294967296 | bytes 4194304 | tf_op jit(solution)/shard_map/merged/pallas_call | solution.py:296
  59.0 3.7 %collective-permute-start.10 = (f32[128,128]{1,0:T(8,128)S(1)}, f32[128,128]{1,0:T(8,128)S(1)}, u32[]{:S(2)}, u32[]{:S(2)}) collective-permute-start(f32[128,128]{1,0:T(8,128)S(1)} %p_own.1.after_ref.refs_1_), channel_id=1, source_target_pairs={{0,24},{4,28},{8,16},{12,20},{16,8},{20,12},{24,0},{28,4},{1,25},{... | collective-permute-start | bytes 196616 | tf_op jit(solution)/shard_map/ppermute | solution.py:532
  62.6 0.8 collective-permute-start.9
  63.4 7.2 %merged.6 = (f32[1024,2048]{1,0:T(8,128)}, f32[8,128]{1,0:T(8,128)S(1)}) custom-call(f32[128,128]{1,0:T(8,128)S(1)} %p_own.1.after_ref.refs_1_, bf16[1024,2048]{1,0:T(8,128)(2,1)S(1)} %get-tuple-element.66.a_ref.refs_7_, bf16[2048,2048]{1,0:T(8,128)(2,1)S(1)} %get-tuple-element.67.e_ref.refs_8_, bf16[1024,2048]{1,0:T(8,128)(2,1)S(1)} %get-tuple-element.52.g_ref.refs_9_), custom_call_target="tpu_custom_call" | custom-call | flops 4294967296 | bytes 4194304 | tf_op jit(solution)/shard_map/merged/pallas_call | solution.py:296
  70.6 1.0 collective-permute-start.11
  71.6 0.6 collective-permute-start.12
  72.2 3.5 %collective-permute-done.11.refs_1_ = f32[1,4,64,128]{3,2,1,0:T(8,128)S(1)} collective-permute-done((f32[1,4,64,128]{3,2,1,0:T(8,128)S(1)}, f32[1,4,64,128]{3,2,1,0:T(8,128)S(1)}, u32[]{:S(2)}, u32[]{:S(2)}) %collective-permute-start.11) | collective-permute-done | bytes 131104 | tf_op jit(solution)/shard_map/ppermute | solution.py:535
  75.7 2.3 %collective-permute-done.12.refs_3_ = f32[1,4,64,128]{3,2,1,0:T(8,128)S(1)} collective-permute-done((f32[1,4,64,128]{3,2,1,0:T(8,128)S(1)}, f32[1,4,64,128]{3,2,1,0:T(8,128)S(1)}, u32[]{:S(2)}, u32[]{:S(2)}) %collective-permute-start.12) | collective-permute-done | bytes 131104 | tf_op jit(solution)/shard_map/ppermute | solution.py:535
  78.1 0.6 collective-permute-start.15
  78.7 1.0 collective-permute-start.17
  79.7 0.2 collective-permute-start.14
  79.9 7.2 %merged.7 = (f32[1024,2048]{1,0:T(8,128)}, f32[8,128]{1,0:T(8,128)S(1)}) custom-call(f32[2,4,64,128]{3,2,1,0:T(8,128)S(1)} %get-tuple-element.71.after_ref.refs_0_, bf16[1024,2048]{1,0:T(8,128)(2,1)S(1)} %get-tuple-element.66.a_ref.refs_7_, bf16[2048,2048]{1,0:T(8,128)(2,1)S(1)} %get-tuple-element.67.e_ref.refs_8_, ...), custom_call_target="tpu_custom_call" | custom-call | flops 4294967296 | bytes 4194304 | tf_op jit(solution)/shard_map/merged/pallas_call | solution.py:296
  87.2 0.3 collective-permute-start.16
  87.5 0.2 collective-permute-start.18
  87.7 4.4 %right_terms.2 = (f32[128,1024]{1,0:T(8,128)S(1)}, f32[128,2048]{1,0:T(8,128)S(1)}, f32[256,256]{1,0:T(8,128)S(1)}) custom-call(s32[3]{0:T(128)S(1)} %pad_add_fusion.ids_ref, f32[8,128]{1,0:T(8,128)S(1)} %get-tuple-element.72.after_ref, f32[2,4,64,128]{3,2,1,0:T(8,128)S(1)} %get-tuple-element.71.after_ref.refs_0_, ...), custom_call_target="tpu_custom_call" | custom-call | flops 3221225472 | bytes 6291456 | tf_op jit(solution)/shard_map/right_terms/pallas_call | solution.py:365
  92.2 5.6 %right_terms.3 = (f32[4,16,2048]{2,1,0:T(8,128)S(1)}, f32[4,16,2048]{2,1,0:T(8,128)S(1)}, f32[128,128]{1,0:T(8,128)S(1)}) custom-call(s32[3]{0:T(128)S(1)} %pad_add_fusion.ids_ref, f32[8,128]{1,0:T(8,128)S(1)} %get-tuple-element.72.after_ref, f32[2,4,64,128]{3,2,1,0:T(8,128)S(1)} %collective-permute-done.13.refs_0_.refs_4_, ...), custom_call_target="tpu_custom_call" | custom-call | flops 3221225472 | bytes 6291456 | tf_op jit(solution)/shard_map/right_terms/pallas_call | solution.py:365
  97.8 0.4 collective-permute-start.19
  98.2 1.6 %collective-permute-done.19.refs_1_ = f32[4,16,2048]{2,1,0:T(8,128)S(1)} collective-permute-done((f32[4,16,2048]{2,1,0:T(8,128)S(1)}, f32[4,16,2048]{2,1,0:T(8,128)S(1)}, u32[]{:S(2)}, u32[]{:S(2)}) %collective-permute-start.19) | collective-permute-done | bytes 524320 | tf_op jit(solution)/shard_map/ppermute | solution.py:529
  99.8 0.1 q_sum.1
  99.8 1.3 collective-permute-start.20
  101.1 3.0 %collective-permute-start.21 = (f32[16,2048]{1,0:T(8,128)S(1)}, f32[16,2048]{1,0:T(8,128)S(1)}, u32[]{:S(2)}, u32[]{:S(2)}) collective-permute-start(f32[16,2048]{1,0:T(8,128)S(1)} %get-tuple-element.82), channel_id=1, source_target_pairs={{0,16},{4,20},{8,24},{12,28},{16,0},{20,4},{24,8},{28,12},{1,17},{... | collective-permute-start | bytes 393224 | tf_op jit(solution)/shard_map/ppermute | solution.py:532
  104.1 0.2 collective-permute-start.22
  104.3 0.0 slice-start.1
  104.4 10.7 %chol_inverse.1.refs_0_.refs_8_ = f32[128,128]{1,0:T(8,128)S(1)} custom-call(f32[16,2048]{1,0:T(8,128)S(1)} %get-tuple-element.79.refs_0_.refs_1_, f32[128,128]{1,0:T(8,128)S(1)} %get-tuple-element.80.refs_1_), custom_call_target="tpu_custom_call" | custom-call | flops 20000000000 | bytes 100000 | tf_op jit(solution)/shard_map/chol_inverse/pallas_call | solution.py:53
  115.1 1.8 %collective-permute-start.23 = (f32[16,2048]{1,0:T(8,128)S(1)}, f32[16,2048]{1,0:T(8,128)S(1)}, u32[]{:S(2)}, u32[]{:S(2)}) collective-permute-start(f32[16,2048]{1,0:T(8,128)S(1)} %q_own.1.after_ref.refs_0_), channel_id=1, source_target_pairs={{0,8},{4,12},{8,0},{12,4},{16,24},{20,28},{24,16},{28,20},{1,9},{5... | collective-permute-start | bytes 393224 | tf_op jit(solution)/shard_map/ppermute | solution.py:532
  116.9 2.5 %collective-permute-start.24 = (f32[16,2048]{1,0:T(8,128)S(1)}, f32[16,2048]{1,0:T(8,128)S(1)}, u32[]{:S(2)}, u32[]{:S(2)}) collective-permute-start(f32[16,2048]{1,0:T(8,128)S(1)} %q_own.1.after_ref.refs_0_), channel_id=1, source_target_pairs={{0,16},{4,20},{8,24},{12,28},{16,0},{20,4},{24,8},{28,12},{1,17},{... | collective-permute-start | bytes 393224 | tf_op jit(solution)/shard_map/ppermute | solution.py:532
  119.4 0.2 collective-permute-start.25
  119.6 2.0 %collective-permute-done.23.refs_1_ = f32[16,2048]{1,0:T(8,128)S(1)} collective-permute-done((f32[16,2048]{1,0:T(8,128)S(1)}, f32[16,2048]{1,0:T(8,128)S(1)}, u32[]{:S(2)}, u32[]{:S(2)}) %collective-permute-start.23) | collective-permute-done | bytes 131104 | tf_op jit(solution)/shard_map/ppermute | solution.py:532
  121.6 7.8 %collective-permute-done.24.refs_2_ = f32[16,2048]{1,0:T(8,128)S(1)} collective-permute-done((f32[16,2048]{1,0:T(8,128)S(1)}, f32[16,2048]{1,0:T(8,128)S(1)}, u32[]{:S(2)}, u32[]{:S(2)}) %collective-permute-start.24) | collective-permute-done | bytes 131104 | tf_op jit(solution)/shard_map/ppermute | solution.py:532
  129.5 0.5 collective-permute-start.29
  130.0 3.4 %left_factor.1.refs_9_ = bf16[4096,256]{1,0:T(8,128)(2,1)S(1)} custom-call(s32[3]{0:T(128)S(1)} %pad_add_fusion.ids_ref, f32[16,2048]{1,0:T(8,128)S(1)} %q_own.1.after_ref.refs_0_, f32[2,4,64,128]{3,2,1,0:T(8,128)S(1)} %get-tuple-element.71.after_ref.refs_0_, f32[2,4,64,128]{3,2,1,0:T(8,128)S(1)} %get-tuple-element.73.refs_1_, ...), custom_call_target="tpu_custom_call" | custom-call | flops 536870912 | bytes 4194304 | tf_op jit(solution)/shard_map/left_factor/pallas_call | solution.py:427
  133.6 16.0 %new_error.1 = (bf16[1,4096,2048]{2,1,0:T(8,128)(2,1)}, f32[2048,128]{1,0:T(8,128)}) custom-call(s32[3]{0:T(128)S(1)} %pad_add_fusion.ids_ref, f32[16,2048]{1,0:T(8,128)S(1)} %q_own.1.after_ref.refs_0_, f32[16,2048]{1,0:T(8,128)S(1)} %collective-permute-done.23.refs_1_, f32[16,2048]{1,0:T(8,128)S(1)} %collective-permute-done.24.refs_2_, ...), custom_call_target="tpu_custom_call" | custom-call | flops 8589934592 | bytes 50331648 | tf_op jit(solution)/shard_map/new_error/pallas_call | solution.py:490
  (52 shorter events, 0.2 us)
Async XLA Ops:
  17.6 11.8 %collective-permute-start = (f32[4,4,128,128]{3,2,1,0:T(8,128)S(1)}, f32[4,4,128,128]{3,2,1,0:T(8,128)S(1)}, u32[]{:S(2)}, u32[]{:S(2)}) collective-permute-start(f32[4,4,128,128]{3,2,1,0:T(8,128)S(1)} %get-tuple-element.48), channel_id=1, source_target_pairs={{0,4},{4,0},{8,12},{12,8},{16,20},{20,16},{24,28},{28,24},{1,5},{5... | collective-permute-start | bytes 3145736 | tf_op jit(solution)/shard_map/ppermute | solution.py:529
  29.6 11.3 %collective-permute-start.1 = (f32[2,4,64,128]{3,2,1,0:T(8,128)S(1)}, f32[2,4,64,128]{3,2,1,0:T(8,128)S(1)}, u32[]{:S(2)}, u32[]{:S(2)}) collective-permute-start(f32[2,4,64,128]{3,2,1,0:T(8,128)S(1)} %get-tuple-element.54), channel_id=1, source_target_pairs={{0,1},{1,0},{2,3},{3,2},{4,5},{5,4},{6,7},{7,6},{8,9},{9,8},{10,11... | collective-permute-start | bytes 786440 | tf_op jit(solution)/shard_map/ppermute | solution.py:535
  32.1 8.8 %collective-permute-start.2 = (f32[2,4,64,128]{3,2,1,0:T(8,128)S(1)}, f32[2,4,64,128]{3,2,1,0:T(8,128)S(1)}, u32[]{:S(2)}, u32[]{:S(2)}) collective-permute-start(f32[2,4,64,128]{3,2,1,0:T(8,128)S(1)} %get-tuple-element.56), channel_id=1, source_target_pairs={{0,2},{1,3},{2,0},{3,1},{4,6},{5,7},{6,4},{7,5},{8,10},{9,11},{10,... | collective-permute-start | bytes 786440 | tf_op jit(solution)/shard_map/ppermute | solution.py:535
  41.0 5.4 %collective-permute-start.3 = (f32[1,4,64,128]{3,2,1,0:T(8,128)S(1)}, f32[1,4,64,128]{3,2,1,0:T(8,128)S(1)}, u32[]{:S(2)}, u32[]{:S(2)}) collective-permute-start(f32[1,4,64,128]{3,2,1,0:T(8,128)S(1)} %get-tuple-element.58), channel_id=1, source_target_pairs={{0,2},{1,3},{2,0},{3,1},{4,6},{5,7},{6,4},{7,5},{8,10},{9,11},{10,... | collective-permute-start | bytes 393224 | tf_op jit(solution)/shard_map/ppermute | solution.py:535
  42.2 5.0 %collective-permute-start.4 = (f32[1,4,64,128]{3,2,1,0:T(8,128)S(1)}, f32[1,4,64,128]{3,2,1,0:T(8,128)S(1)}, u32[]{:S(2)}, u32[]{:S(2)}) collective-permute-start(f32[1,4,64,128]{3,2,1,0:T(8,128)S(1)} %get-tuple-element.60), channel_id=1, source_target_pairs={{0,1},{1,0},{2,3},{3,2},{4,5},{5,4},{6,7},{7,6},{8,9},{9,8},{10,11... | collective-permute-start | bytes 393224 | tf_op jit(solution)/shard_map/ppermute | solution.py:535
  47.2 11.7 %collective-permute-start.5 = (f32[128,128]{1,0:T(8,128)S(1)}, f32[128,128]{1,0:T(8,128)S(1)}, u32[]{:S(2)}, u32[]{:S(2)}) collective-permute-start(f32[128,128]{1,0:T(8,128)S(1)} %get-tuple-element.63), channel_id=1, source_target_pairs={{0,8},{4,12},{8,0},{12,4},{16,24},{20,28},{24,16},{28,20},{1,9},{5... | collective-permute-start | bytes 196616 | tf_op jit(solution)/shard_map/ppermute | solution.py:532
  48.9 10.1 %collective-permute-start.6 = (f32[128,128]{1,0:T(8,128)S(1)}, f32[128,128]{1,0:T(8,128)S(1)}, u32[]{:S(2)}, u32[]{:S(2)}) collective-permute-start(f32[128,128]{1,0:T(8,128)S(1)} %get-tuple-element.64), channel_id=1, source_target_pairs={{0,16},{4,20},{8,24},{12,28},{16,0},{20,4},{24,8},{28,12},{1,17},{... | collective-permute-start | bytes 196616 | tf_op jit(solution)/shard_map/ppermute | solution.py:532
  51.4 7.5 %collective-permute-start.7 = (f32[128,128]{1,0:T(8,128)S(1)}, f32[128,128]{1,0:T(8,128)S(1)}, u32[]{:S(2)}, u32[]{:S(2)}) collective-permute-start(f32[128,128]{1,0:T(8,128)S(1)} %get-tuple-element.65), channel_id=1, source_target_pairs={{0,24},{4,28},{8,16},{12,20},{16,8},{20,12},{24,0},{28,4},{1,25},{... | collective-permute-start | bytes 196616 | tf_op jit(solution)/shard_map/ppermute | solution.py:532
  59.0 11.6 %collective-permute-start.10 = (f32[128,128]{1,0:T(8,128)S(1)}, f32[128,128]{1,0:T(8,128)S(1)}, u32[]{:S(2)}, u32[]{:S(2)}) collective-permute-start(f32[128,128]{1,0:T(8,128)S(1)} %p_own.1.after_ref.refs_1_), channel_id=1, source_target_pairs={{0,24},{4,28},{8,16},{12,20},{16,8},{20,12},{24,0},{28,4},{1,25},{... | collective-permute-start | bytes 196616 | tf_op jit(solution)/shard_map/ppermute | solution.py:532
  62.6 8.0 %collective-permute-start.8 = (f32[128,128]{1,0:T(8,128)S(1)}, f32[128,128]{1,0:T(8,128)S(1)}, u32[]{:S(2)}, u32[]{:S(2)}) collective-permute-start(f32[128,128]{1,0:T(8,128)S(1)} %p_own.1.after_ref.refs_1_), channel_id=1, source_target_pairs={{0,8},{4,12},{8,0},{12,4},{16,24},{20,28},{24,16},{28,20},{1,9},{5... | collective-permute-start | bytes 196616 | tf_op jit(solution)/shard_map/ppermute | solution.py:532
  62.6 8.0 %collective-permute-start.9 = (f32[128,128]{1,0:T(8,128)S(1)}, f32[128,128]{1,0:T(8,128)S(1)}, u32[]{:S(2)}, u32[]{:S(2)}) collective-permute-start(f32[128,128]{1,0:T(8,128)S(1)} %p_own.1.after_ref.refs_1_), channel_id=1, source_target_pairs={{0,16},{4,20},{8,24},{12,28},{16,0},{20,4},{24,8},{28,12},{1,17},{... | collective-permute-start | bytes 196616 | tf_op jit(solution)/shard_map/ppermute | solution.py:532
  70.6 5.0 %collective-permute-start.11 = (f32[1,4,64,128]{3,2,1,0:T(8,128)S(1)}, f32[1,4,64,128]{3,2,1,0:T(8,128)S(1)}, u32[]{:S(2)}, u32[]{:S(2)}) collective-permute-start(f32[1,4,64,128]{3,2,1,0:T(8,128)S(1)} %get-tuple-element.69.refs_0_), channel_id=1, source_target_pairs={{0,2},{1,3},{2,0},{3,1},{4,6},{5,7},{6,4},{7,5},{8,10},{9,11},{10,... | collective-permute-start | bytes 393224 | tf_op jit(solution)/shard_map/ppermute | solution.py:535
  71.6 6.4 %collective-permute-start.12 = (f32[1,4,64,128]{3,2,1,0:T(8,128)S(1)}, f32[1,4,64,128]{3,2,1,0:T(8,128)S(1)}, u32[]{:S(2)}, u32[]{:S(2)}) collective-permute-start(f32[1,4,64,128]{3,2,1,0:T(8,128)S(1)} %get-tuple-element.70.refs_2_), channel_id=1, source_target_pairs={{0,1},{1,0},{2,3},{3,2},{4,5},{5,4},{6,7},{7,6},{8,9},{9,8},{10,11... | collective-permute-start | bytes 393224 | tf_op jit(solution)/shard_map/ppermute | solution.py:535
  78.1 9.1 %collective-permute-start.15 = (f32[2,4,64,128]{3,2,1,0:T(8,128)S(1)}, f32[2,4,64,128]{3,2,1,0:T(8,128)S(1)}, u32[]{:S(2)}, u32[]{:S(2)}) collective-permute-start(f32[2,4,64,128]{3,2,1,0:T(8,128)S(1)} %get-tuple-element.71.after_ref.refs_0_), channel_id=1, source_target_pairs={{0,1},{1,0},{2,3},{3,2},{4,5},{5,4},{6,7},{7,6},{8,9},{9,8},{10,11... | collective-permute-start | bytes 786440 | tf_op jit(solution)/shard_map/ppermute | solution.py:535
  78.7 13.4 %collective-permute-start.13 = (f32[2,4,64,128]{3,2,1,0:T(8,128)S(1)}, f32[2,4,64,128]{3,2,1,0:T(8,128)S(1)}, u32[]{:S(2)}, u32[]{:S(2)}) collective-permute-start(f32[2,4,64,128]{3,2,1,0:T(8,128)S(1)} %get-tuple-element.71.after_ref.refs_0_), channel_id=1, source_target_pairs={{0,4},{4,0},{8,12},{12,8},{16,20},{20,16},{24,28},{28,24},{1,5},{5... | collective-permute-start | bytes 786440 | tf_op jit(solution)/shard_map/ppermute | solution.py:529
  78.7 8.8 %collective-permute-start.17 = (f32[2,4,64,128]{3,2,1,0:T(8,128)S(1)}, f32[2,4,64,128]{3,2,1,0:T(8,128)S(1)}, u32[]{:S(2)}, u32[]{:S(2)}) collective-permute-start(f32[2,4,64,128]{3,2,1,0:T(8,128)S(1)} %get-tuple-element.73.refs_1_), channel_id=1, source_target_pairs={{0,2},{1,3},{2,0},{3,1},{4,6},{5,7},{6,4},{7,5},{8,10},{9,11},{10,... | collective-permute-start | bytes 786440 | tf_op jit(solution)/shard_map/ppermute | solution.py:535
  79.7 12.4 %collective-permute-start.14 = (f32[2,4,64,128]{3,2,1,0:T(8,128)S(1)}, f32[2,4,64,128]{3,2,1,0:T(8,128)S(1)}, u32[]{:S(2)}, u32[]{:S(2)}) collective-permute-start(f32[2,4,64,128]{3,2,1,0:T(8,128)S(1)} %get-tuple-element.73.refs_1_), channel_id=1, source_target_pairs={{0,4},{4,0},{8,12},{12,8},{16,20},{20,16},{24,28},{28,24},{1,5},{5... | collective-permute-start | bytes 786440 | tf_op jit(solution)/shard_map/ppermute | solution.py:529
  87.2 5.0 %collective-permute-start.16 = (f32[2,4,64,128]{3,2,1,0:T(8,128)S(1)}, f32[2,4,64,128]{3,2,1,0:T(8,128)S(1)}, u32[]{:S(2)}, u32[]{:S(2)}) collective-permute-start(f32[2,4,64,128]{3,2,1,0:T(8,128)S(1)} %collective-permute-done.15.refs_2_), channel_id=1, source_target_pairs={{0,4},{4,0},{8,12},{12,8},{16,20},{20,16},{24,28},{28,24},{1,5},{5... | collective-permute-start | bytes 786440 | tf_op jit(solution)/shard_map/ppermute | solution.py:529
  87.5 4.7 %collective-permute-start.18 = (f32[2,4,64,128]{3,2,1,0:T(8,128)S(1)}, f32[2,4,64,128]{3,2,1,0:T(8,128)S(1)}, u32[]{:S(2)}, u32[]{:S(2)}) collective-permute-start(f32[2,4,64,128]{3,2,1,0:T(8,128)S(1)} %collective-permute-done.17.refs_3_), channel_id=1, source_target_pairs={{0,4},{4,0},{8,12},{12,8},{16,20},{20,16},{24,28},{28,24},{1,5},{5... | collective-permute-start | bytes 786440 | tf_op jit(solution)/shard_map/ppermute | solution.py:529
  97.8 2.0 %collective-permute-start.19 = (f32[4,16,2048]{2,1,0:T(8,128)S(1)}, f32[4,16,2048]{2,1,0:T(8,128)S(1)}, u32[]{:S(2)}, u32[]{:S(2)}) collective-permute-start(f32[4,16,2048]{2,1,0:T(8,128)S(1)} %get-tuple-element.78), channel_id=1, source_target_pairs={{0,4},{4,0},{8,12},{12,8},{16,20},{20,16},{24,28},{28,24},{1,5},{5... | collective-permute-start | bytes 1572872 | tf_op jit(solution)/shard_map/ppermute | solution.py:529
  99.8 15.2 %collective-permute-start.20 = (f32[16,2048]{1,0:T(8,128)S(1)}, f32[16,2048]{1,0:T(8,128)S(1)}, u32[]{:S(2)}, u32[]{:S(2)}) collective-permute-start(f32[16,2048]{1,0:T(8,128)S(1)} %get-tuple-element.81), channel_id=1, source_target_pairs={{0,8},{4,12},{8,0},{12,4},{16,24},{20,28},{24,16},{28,20},{1,9},{5... | collective-permute-start | bytes 393224 | tf_op jit(solution)/shard_map/ppermute | solution.py:532
  101.1 14.0 %collective-permute-start.21 = (f32[16,2048]{1,0:T(8,128)S(1)}, f32[16,2048]{1,0:T(8,128)S(1)}, u32[]{:S(2)}, u32[]{:S(2)}) collective-permute-start(f32[16,2048]{1,0:T(8,128)S(1)} %get-tuple-element.82), channel_id=1, source_target_pairs={{0,16},{4,20},{8,24},{12,28},{16,0},{20,4},{24,8},{28,12},{1,17},{... | collective-permute-start | bytes 393224 | tf_op jit(solution)/shard_map/ppermute | solution.py:532
  104.1 11.0 %collective-permute-start.22 = (f32[16,2048]{1,0:T(8,128)S(1)}, f32[16,2048]{1,0:T(8,128)S(1)}, u32[]{:S(2)}, u32[]{:S(2)}) collective-permute-start(f32[16,2048]{1,0:T(8,128)S(1)} %get-tuple-element.83), channel_id=1, source_target_pairs={{0,24},{4,28},{8,16},{12,20},{16,8},{20,12},{24,0},{28,4},{1,25},{... | collective-permute-start | bytes 393224 | tf_op jit(solution)/shard_map/ppermute | solution.py:532
  104.3 29.2 %slice-start = ((s8[8388608]{0:T(1024)(128)(4,1)}), s8[4194304]{0:T(1024)(128)(4,1)S(1)}, s32[]{:S(2)}) async-start(s8[8388608]{0:T(1024)(128)(4,1)} %bitcast.6), calls=%async_computation | async-start | bytes 8388608
  104.3 29.2 %slice-start.2 = ((s8[8388608]{0:T(1024)(128)(4,1)}), s8[4194304]{0:T(1024)(128)(4,1)S(1)}, s32[]{:S(2)}) async-start(s8[8388608]{0:T(1024)(128)(4,1)} %bitcast.8), calls=%async_computation.2 | async-start | bytes 8388608
  104.3 29.2 %slice-start.4 = ((s8[8388608]{0:T(1024)(128)(4,1)}), s8[4194304]{0:T(1024)(128)(4,1)S(1)}, s32[]{:S(2)}) async-start(s8[8388608]{0:T(1024)(128)(4,1)} %bitcast.10), calls=%async_computation.4 | async-start | bytes 8388608
  104.3 29.2 %slice-start.6 = ((s8[8388608]{0:T(1024)(128)(4,1)}), s8[4194304]{0:T(1024)(128)(4,1)S(1)}, s32[]{:S(2)}) async-start(s8[8388608]{0:T(1024)(128)(4,1)} %bitcast.12), calls=%async_computation.6 | async-start | bytes 8388608
  104.3 29.2 %slice-start.1 = ((s8[8388608]{0:T(1024)(128)(4,1)}), s8[4194304]{0:T(1024)(128)(4,1)S(1)}, s32[]{:S(2)}) async-start(s8[8388608]{0:T(1024)(128)(4,1)} %bitcast.6), calls=%async_computation.1 | async-start | bytes 8388608
  104.3 29.2 %slice-start.3 = ((s8[8388608]{0:T(1024)(128)(4,1)}), s8[4194304]{0:T(1024)(128)(4,1)S(1)}, s32[]{:S(2)}) async-start(s8[8388608]{0:T(1024)(128)(4,1)} %bitcast.8), calls=%async_computation.3 | async-start | bytes 8388608
  104.3 29.2 %slice-start.5 = ((s8[8388608]{0:T(1024)(128)(4,1)}), s8[4194304]{0:T(1024)(128)(4,1)S(1)}, s32[]{:S(2)}) async-start(s8[8388608]{0:T(1024)(128)(4,1)} %bitcast.10), calls=%async_computation.5 | async-start | bytes 8388608
  104.3 29.2 %slice-start.7 = ((s8[8388608]{0:T(1024)(128)(4,1)}), s8[4194304]{0:T(1024)(128)(4,1)S(1)}, s32[]{:S(2)}) async-start(s8[8388608]{0:T(1024)(128)(4,1)} %bitcast.12), calls=%async_computation.7 | async-start | bytes 8388608
  115.1 6.5 %collective-permute-start.23 = (f32[16,2048]{1,0:T(8,128)S(1)}, f32[16,2048]{1,0:T(8,128)S(1)}, u32[]{:S(2)}, u32[]{:S(2)}) collective-permute-start(f32[16,2048]{1,0:T(8,128)S(1)} %q_own.1.after_ref.refs_0_), channel_id=1, source_target_pairs={{0,8},{4,12},{8,0},{12,4},{16,24},{20,28},{24,16},{28,20},{1,9},{5... | collective-permute-start | bytes 393224 | tf_op jit(solution)/shard_map/ppermute | solution.py:532
  116.9 12.6 %collective-permute-start.24 = (f32[16,2048]{1,0:T(8,128)S(1)}, f32[16,2048]{1,0:T(8,128)S(1)}, u32[]{:S(2)}, u32[]{:S(2)}) collective-permute-start(f32[16,2048]{1,0:T(8,128)S(1)} %q_own.1.after_ref.refs_0_), channel_id=1, source_target_pairs={{0,16},{4,20},{8,24},{12,28},{16,0},{20,4},{24,8},{28,12},{1,17},{... | collective-permute-start | bytes 393224 | tf_op jit(solution)/shard_map/ppermute | solution.py:532
  119.4 10.1 %collective-permute-start.25 = (f32[16,2048]{1,0:T(8,128)S(1)}, f32[16,2048]{1,0:T(8,128)S(1)}, u32[]{:S(2)}, u32[]{:S(2)}) collective-permute-start(f32[16,2048]{1,0:T(8,128)S(1)} %q_own.1.after_ref.refs_0_), channel_id=1, source_target_pairs={{0,24},{4,28},{8,16},{12,20},{16,8},{20,12},{24,0},{28,4},{1,25},{... | collective-permute-start | bytes 393224 | tf_op jit(solution)/shard_map/ppermute | solution.py:532
  119.6 13.8 %collective-permute-start.26 = (f32[16,2048]{1,0:T(8,128)S(1)}, f32[16,2048]{1,0:T(8,128)S(1)}, u32[]{:S(2)}, u32[]{:S(2)}) collective-permute-start(f32[16,2048]{1,0:T(8,128)S(1)} %q_own.1.after_ref.refs_0_), channel_id=1, source_target_pairs={{0,4},{4,0},{8,12},{12,8},{16,20},{20,16},{24,28},{28,24},{1,5},{5... | collective-permute-start | bytes 393224 | tf_op jit(solution)/shard_map/ppermute | solution.py:529
  121.6 11.8 %collective-permute-start.27 = (f32[16,2048]{1,0:T(8,128)S(1)}, f32[16,2048]{1,0:T(8,128)S(1)}, u32[]{:S(2)}, u32[]{:S(2)}) collective-permute-start(f32[16,2048]{1,0:T(8,128)S(1)} %collective-permute-done.23.refs_1_), channel_id=1, source_target_pairs={{0,4},{4,0},{8,12},{12,8},{16,20},{20,16},{24,28},{28,24},{1,5},{5... | collective-permute-start | bytes 393224 | tf_op jit(solution)/shard_map/ppermute | solution.py:529
  129.5 4.0 %collective-permute-start.28 = (f32[16,2048]{1,0:T(8,128)S(1)}, f32[16,2048]{1,0:T(8,128)S(1)}, u32[]{:S(2)}, u32[]{:S(2)}) collective-permute-start(f32[16,2048]{1,0:T(8,128)S(1)} %collective-permute-done.24.refs_2_), channel_id=1, source_target_pairs={{0,4},{4,0},{8,12},{12,8},{16,20},{20,16},{24,28},{28,24},{1,5},{5... | collective-permute-start | bytes 393224 | tf_op jit(solution)/shard_map/ppermute | solution.py:529
  129.5 4.0 %collective-permute-start.29 = (f32[16,2048]{1,0:T(8,128)S(1)}, f32[16,2048]{1,0:T(8,128)S(1)}, u32[]{:S(2)}, u32[]{:S(2)}) collective-permute-start(f32[16,2048]{1,0:T(8,128)S(1)} %collective-permute-done.25.refs_3_), channel_id=1, source_target_pairs={{0,4},{4,0},{8,12},{12,8},{16,20},{20,16},{24,28},{28,24},{1,5},{5... | collective-permute-start | bytes 393224 | tf_op jit(solution)/shard_map/ppermute | solution.py:529
